TPU v7x, 128 devices: a whole 4x4x4 slice. The times are simulated.
128 devices in a mesh: section: 2 (over y_lo), dp: 32 (over y_hi, z, x), tensor: 2 (over core).
Axes of the slice: x: 4, y: 4 (y_hi: 2, y_lo: 2; y = y_hi * 2 + y_lo), z: 4, core: 2. Of those that a mesh axis runs over, the one named last changes fastest.
Arguments:
- block_input: bfloat16 [2, 16384, 512], P(None, ('dp', 'tensor')), may hold values from -6 to 6
- out_cotangent: bfloat16 [2, 16384, 512], P(None, ('dp', 'tensor')), may hold values from -6 to 6
- segments: int32 [2, 16384], P(None, 'dp'), may hold values from 0 to 255, as said below
- positions: int32 [2, 16384], P(None, 'dp'), may hold values from 0 to 1535, as said below
- norm_gains: bfloat16 [2, 2, 512], P('section', None, ('dp', 'tensor')), may hold values from 0.099609375 to 1.8984375
- norm_shifts: bfloat16 [2, 2, 512], P('section', None, ('dp', 'tensor')), may hold values from -3 to 3
- inward_weight: bfloat16 [2, 512, 3, 512], P('section', 'dp', None, 'tensor'), may hold values from -0.25 to 0.25
- inward_bias: bfloat16 [2, 3, 8, 64], P('section', None, 'tensor', 'dp'), may hold values from -3 to 3
- outward_weight: bfloat16 [2, 512, 512], P('section', 'tensor', 'dp'), may hold values from -1 to 1
- outward_bias: bfloat16 [2, 512], P('section', ('dp', 'tensor')), may hold values from -3 to 3
- expand_weight: bfloat16 [2, 512, 2048], P('section', 'dp', 'tensor'), may hold values from -0.25 to 0.25
- expand_bias: bfloat16 [2, 16, 128], P('section', 'tensor', 'dp'), may hold values from -3 to 3
- shrink_weight: bfloat16 [2, 2048, 512], P('section', 'tensor', 'dp'), may hold values from -0.125 to 0.125
- shrink_bias: bfloat16 [2, 512], P('section', ('dp', 'tensor')), may hold values from -3 to 3
Outputs:
- hidden_states: bfloat16 [2, 2, 16384, 512], P('section', None, ('dp', 'tensor'))
- input_grads: float32 [2, 2, 16384, 512], P('section', None, ('dp', 'tensor'))
- gains_grad: float32 [2, 2, 512], P('section', None, ('dp', 'tensor'))
- shifts_grad: float32 [2, 2, 512], P('section', None, ('dp', 'tensor'))
- inward_weight_grad: float32 [2, 512, 3, 512], P('section', 'dp', None, 'tensor')
- inward_bias_grad: float32 [2, 3, 8, 64], P('section', None, 'tensor', 'dp')
- outward_weight_grad: float32 [2, 512, 512], P('section', 'tensor', 'dp')
- outward_bias_grad: float32 [2, 512], P('section', ('dp', 'tensor'))
- expand_weight_grad: float32 [2, 512, 2048], P('section', 'dp', 'tensor')
- expand_bias_grad: float32 [2, 16, 128], P('section', 'tensor', 'dp')
- shrink_weight_grad: float32 [2, 2048, 512], P('section', 'tensor', 'dp')
- shrink_bias_grad: float32 [2, 512], P('section', ('dp', 'tensor'))
Inputs may be any that keep to these rules, and one draw needn't show every extreme that they name: `segments`: document numbers never fall along the tokens, and tokens of different packed sequences of 512 tokens have different numbers. Within a document the positions rise by one from token to token.
All inputs are finite; a program needn't handle non-finite values.
Results may differ from a plain program's by a relative error of at most 0.025.
Values may be sent and summed in bfloat16 or wider, within the bound.
A program may use at most 128 MiB of HBM per device.

v0:
```python
import jax
import jax.numpy as jnp
from jax import lax
from jax.sharding import PartitionSpec as P

HD = 64
ROT = 16
LEN = 512


EPSILON = 1e-05
MASKED = -1e30


def passed_along(array, axis, by):
    length = lax.axis_size(axis)
    pairs = [(i, i + by) for i in range(length) if 0 <= i + by < length]
    return lax.ppermute(array, axis, pairs)


def norm_rows(values, gain, shift):
    center = values - jnp.mean(values, axis=-1, keepdims=True)
    spread = jnp.mean(center * center, axis=-1, keepdims=True)
    return center * lax.rsqrt(spread + EPSILON) * gain + shift


def turning(places):
    steps_half = jnp.arange(ROT // 2).astype(jnp.float32)
    rates = 10000.0 ** (-2.0 * steps_half / ROT)
    angles = places.astype(jnp.float32)[:, None] * rates[None, :]
    return (jnp.cos(angles)[:, None, :], jnp.sin(angles)[:, None, :])


def rotate(values, cosine, sine_part):
    half_rot = ROT // 2
    front = values[..., :half_rot]
    behind = values[..., half_rot:ROT]
    return jnp.concatenate(
        [
            front * cosine - behind * sine_part,
            behind * cosine + front * sine_part,
            values[..., ROT:],
        ],
        axis=-1,
    )


def allowed_pairs(labels):
    places = jnp.arange(LEN)
    return (labels[:, None] == labels[None, :]) & (places[None, :] <= places[:, None])


def gelu_exact(values):
    return jax.nn.gelu(values, approximate=False)


def outer_rows(left, right):
    return lax.dot_general(
        left, right, (((0,), (0,)), ((), ())), preferred_element_type=jnp.float32
    )


def inner_cols(left, right):
    return lax.dot_general(
        left, right, (((1,), (1,)), ((), ())), preferred_element_type=jnp.float32
    )


def attend_forward(queries, keys_rot, values, labels):
    shape_seq = (-1, LEN, queries.shape[1], HD)

    def one_block(block_args):
        block_query, block_key, block_value, block_labels = block_args
        scores = jnp.einsum(
            "qhd,khd->hqk", block_query, block_key, preferred_element_type=jnp.float32
        ) * HD ** (-0.5)
        scores = jnp.where(allowed_pairs(block_labels)[None], scores, MASKED)
        row_max = jnp.max(scores, axis=-1, keepdims=True)
        powers = jnp.exp(scores - row_max)
        row_total = jnp.sum(powers, axis=-1, keepdims=True)
        shares = (powers / row_total).astype(jnp.bfloat16)
        block_mixed = jnp.einsum(
            "hqk,khd->qhd", shares, block_value, preferred_element_type=jnp.float32
        )
        return (block_mixed, (row_max + jnp.log(row_total))[..., 0])

    mixed, logsum = lax.map(
        one_block,
        (
            queries.reshape(shape_seq),
            keys_rot.reshape(shape_seq),
            values.reshape(shape_seq),
            labels.reshape(-1, LEN),
        ),
    )
    return (mixed.reshape(queries.shape[0], -1), logsum)


def attend_backward(queries, keys_rot, values, grad_mixed, logsum, labels):
    shape_seq = (-1, LEN, queries.shape[1], HD)
    score_scale = HD ** (-0.5)

    def one_block(block_args):
        block_query, block_key, block_value, block_grad, block_sum, block_labels = block_args
        scores = (
            jnp.einsum("qhd,khd->hqk", block_query, block_key, preferred_element_type=jnp.float32)
            * score_scale
        )
        allowed = allowed_pairs(block_labels)[None]
        shares = jnp.where(allowed, jnp.exp(scores - block_sum[..., None]), 0.0)
        grad_shares = jnp.einsum(
            "qhd,khd->hqk", block_grad, block_value, preferred_element_type=jnp.float32
        )
        row_dot = jnp.sum(grad_shares * shares, axis=-1, keepdims=True)
        grad_scores = (shares * (grad_shares - row_dot)).astype(jnp.bfloat16)
        grad_query = (
            jnp.einsum("hqk,khd->qhd", grad_scores, block_key, preferred_element_type=jnp.float32)
            * score_scale
        )
        grad_key = (
            jnp.einsum("hqk,qhd->khd", grad_scores, block_query, preferred_element_type=jnp.float32)
            * score_scale
        )
        grad_value = jnp.einsum(
            "hqk,qhd->khd",
            shares.astype(jnp.bfloat16),
            block_grad,
            preferred_element_type=jnp.float32,
        )
        return (grad_query, grad_key, grad_value)

    block_grads = lax.map(
        one_block,
        (
            queries.reshape(shape_seq),
            keys_rot.reshape(shape_seq),
            values.reshape(shape_seq),
            grad_mixed.reshape(shape_seq),
            logsum,
            labels.reshape(-1, LEN),
        ),
    )
    return tuple((member.reshape(queries.shape) for member in block_grads))


def forward_layer(entry_rows, gathered, vectors, labels, places):
    inward, outward, expand, shrink, inward_shift, expand_shift = gathered
    gains, shifts, outward_shift, shrink_shift = vectors
    first = norm_rows(entry_rows, gains[0], shifts[0]).astype(jnp.bfloat16)
    second = norm_rows(entry_rows, gains[1], shifts[1]).astype(jnp.bfloat16)
    first_all, second_all = (
        lax.all_gather(first, "tensor", axis=0, tiled=True),
        lax.all_gather(second, "tensor", axis=0, tiled=True),
    )
    row_count = first_all.shape[0]
    head_count = inward_shift.shape[1]
    joint = jnp.dot(
        first_all, inward.reshape(inward.shape[0], -1), preferred_element_type=jnp.float32
    ) + inward_shift.astype(jnp.float32).reshape(-1)
    joint = joint.reshape(row_count, 3, head_count, HD)
    cosine, sine_part = turning(places)
    queries = rotate(joint[:, 0], cosine, sine_part).astype(jnp.bfloat16)
    keys_rot = rotate(joint[:, 1], cosine, sine_part).astype(jnp.bfloat16)
    values = joint[:, 2].astype(jnp.bfloat16)
    mixed, logsum = attend_forward(queries, keys_rot, values, labels)
    mixed = mixed.astype(jnp.bfloat16)
    before = jnp.dot(second_all, expand, preferred_element_type=jnp.float32) + expand_shift.astype(
        jnp.float32
    ).reshape(-1)
    hidden = gelu_exact(before).astype(jnp.bfloat16)
    branch = jnp.dot(mixed, outward, preferred_element_type=jnp.float32) + jnp.dot(
        hidden, shrink, preferred_element_type=jnp.float32
    )
    branch = lax.psum_scatter(branch, "tensor", scatter_dimension=0, tiled=True)
    result = entry_rows + branch + outward_shift + shrink_shift
    return (
        result,
        (
            entry_rows,
            first_all,
            second_all,
            queries,
            keys_rot,
            values,
            logsum,
            mixed,
            before,
            hidden,
        ),
    )


def backward_layer(grad_out, kept_state, gathered, vectors, labels, places):
    entry_rows, first_all, second_all, queries, keys_rot, values, logsum, mixed, before, hidden = (
        kept_state
    )
    inward, outward, expand, shrink, inward_shift, expand_shift = gathered
    gains, shifts, outward_shift, shrink_shift = vectors
    bias_sum = jnp.sum(grad_out, axis=0)
    grad_all = lax.all_gather(grad_out.astype(jnp.bfloat16), "tensor", axis=0, tiled=True)
    grad_outward = outer_rows(mixed, grad_all)
    grad_shrink = outer_rows(hidden, grad_all)
    grad_mixed = inner_cols(grad_all, outward).astype(jnp.bfloat16)
    grad_hidden = inner_cols(grad_all, shrink)
    gelu_value, gelu_pull = jax.vjp(gelu_exact, before)
    grad_before = gelu_pull(grad_hidden)[0].astype(jnp.bfloat16)
    grad_expand_shift = jnp.sum(grad_before, axis=0, dtype=jnp.float32)
    grad_expand = outer_rows(second_all, grad_before)
    grad_second = inner_cols(grad_before, expand)
    grad_query, grad_key, grad_value = attend_backward(
        queries, keys_rot, values, grad_mixed.reshape(queries.shape), logsum, labels
    )
    cosine, sine_part = turning(places)
    grad_joint = jnp.stack(
        [rotate(grad_query, cosine, -sine_part), rotate(grad_key, cosine, -sine_part), grad_value],
        axis=1,
    ).astype(jnp.bfloat16)
    grad_inward_shift = jnp.sum(grad_joint, axis=0, dtype=jnp.float32)
    flat_joint = grad_joint.reshape(grad_joint.shape[0], -1)
    grad_inward = outer_rows(first_all, flat_joint).reshape(inward.shape)
    grad_first = inner_cols(flat_joint, inward.reshape(inward.shape[0], -1))
    grad_first, grad_second = (
        lax.psum_scatter(grad_first, "tensor", scatter_dimension=0, tiled=True),
        lax.psum_scatter(grad_second, "tensor", scatter_dimension=0, tiled=True),
    )
    norm_one, pull_one = jax.vjp(norm_rows, entry_rows, gains[0], shifts[0])
    norm_two, pull_two = jax.vjp(norm_rows, entry_rows, gains[1], shifts[1])
    back_one = pull_one(grad_first)
    back_two = pull_two(grad_second)
    grad_entry = grad_out + back_one[0] + back_two[0]
    weight_terms = (
        grad_inward,
        grad_outward,
        grad_expand,
        grad_shrink,
        grad_inward_shift,
        grad_expand_shift.reshape(expand_shift.shape),
    )
    vector_terms = (
        jnp.stack([back_one[1], back_two[1]]),
        jnp.stack([back_one[2], back_two[2]]),
        bias_sum,
        bias_sum,
    )
    return (grad_entry, weight_terms, vector_terms)


def local(
    block_input,
    out_cotangent,
    segments,
    positions,
    norm_gains,
    norm_shifts,
    inward_weight,
    inward_bias,
    outward_weight,
    outward_bias,
    expand_weight,
    expand_bias,
    shrink_weight,
    shrink_bias,
):
    section_count = lax.axis_size("section")
    section_index = lax.axis_index("section")
    micro_count = block_input.shape[0]
    tick_count = micro_count + section_count - 1
    pieces = (
        inward_weight[0],
        outward_weight[0],
        expand_weight[0],
        shrink_weight[0],
        inward_bias[0],
        expand_bias[0],
    )
    gathered = (
        lax.all_gather(pieces[0], "dp", axis=0, tiled=True),
        lax.all_gather(pieces[1], "dp", axis=1, tiled=True),
        lax.all_gather(pieces[2], "dp", axis=0, tiled=True),
        lax.all_gather(pieces[3], "dp", axis=1, tiled=True),
        lax.all_gather(pieces[4], "dp", axis=2, tiled=True),
        lax.all_gather(pieces[5], "dp", axis=1, tiled=True),
    )
    vectors = (
        lax.all_gather(norm_gains[0], ("dp", "tensor"), axis=1, tiled=True),
        lax.all_gather(norm_shifts[0], ("dp", "tensor"), axis=1, tiled=True),
        lax.all_gather(outward_bias[0], ("dp", "tensor"), axis=0, tiled=True),
        lax.all_gather(shrink_bias[0], ("dp", "tensor"), axis=0, tiled=True),
    )
    vectors = tuple((member.astype(jnp.float32) for member in vectors))
    received = jnp.zeros(block_input.shape[1:], jnp.bfloat16)
    kept_states = []
    sent_rows = []
    for moment in range(tick_count):
        own_rows = block_input[min(moment, micro_count - 1)]
        entry_rows = jnp.where(section_index == 0, own_rows, received).astype(jnp.float32)
        batch_at = jnp.clip(moment - section_index, 0, micro_count - 1)
        labels = lax.dynamic_index_in_dim(segments, batch_at, 0, keepdims=False)
        places = lax.dynamic_index_in_dim(positions, batch_at, 0, keepdims=False)
        result, kept_state = forward_layer(entry_rows, gathered, vectors, labels, places)
        outgoing = result.astype(jnp.bfloat16)
        sent_rows.append(outgoing)
        kept_states.append(kept_state)
        if moment + 1 < tick_count:
            received = passed_along(outgoing, "section", 1)
    gathered = (
        lax.all_gather(pieces[0], "dp", axis=0, tiled=True),
        lax.all_gather(pieces[1], "dp", axis=1, tiled=True),
        lax.all_gather(pieces[2], "dp", axis=0, tiled=True),
        lax.all_gather(pieces[3], "dp", axis=1, tiled=True),
        lax.all_gather(pieces[4], "dp", axis=2, tiled=True),
        lax.all_gather(pieces[5], "dp", axis=1, tiled=True),
    )
    back_rows = jnp.zeros(block_input.shape[1:], jnp.bfloat16)
    weight_sums = None
    vector_sums = None
    entry_grads = []
    for moment in range(tick_count - 1, -1, -1):
        batch_raw = moment - section_index
        live = (batch_raw >= 0) & (batch_raw < micro_count)
        batch_at = jnp.clip(batch_raw, 0, micro_count - 1)
        given = lax.dynamic_index_in_dim(out_cotangent, batch_at, 0, keepdims=False)
        incoming = jnp.where(section_index == section_count - 1, given, back_rows).astype(
            jnp.float32
        )
        incoming = jnp.where(live, incoming, 0.0)
        labels = lax.dynamic_index_in_dim(segments, batch_at, 0, keepdims=False)
        places = lax.dynamic_index_in_dim(positions, batch_at, 0, keepdims=False)
        grad_entry, weight_terms, vector_terms = backward_layer(
            incoming, kept_states[moment], gathered, vectors, labels, places
        )
        weight_sums = (
            weight_terms
            if weight_sums is None
            else jax.tree.map(jnp.add, weight_sums, weight_terms)
        )
        vector_sums = (
            vector_terms
            if vector_sums is None
            else jax.tree.map(jnp.add, vector_sums, vector_terms)
        )
        entry_grads.append(grad_entry)
        if moment > 0:
            back_rows = passed_along(grad_entry.astype(jnp.bfloat16), "section", -1)
    weight_sums = (
        lax.psum_scatter(
            weight_sums[0].astype(jnp.bfloat16), "dp", scatter_dimension=0, tiled=True
        ).astype(jnp.float32),
        lax.psum_scatter(
            weight_sums[1].astype(jnp.bfloat16), "dp", scatter_dimension=1, tiled=True
        ).astype(jnp.float32),
        lax.psum_scatter(
            weight_sums[2].astype(jnp.bfloat16), "dp", scatter_dimension=0, tiled=True
        ).astype(jnp.float32),
        lax.psum_scatter(
            weight_sums[3].astype(jnp.bfloat16), "dp", scatter_dimension=1, tiled=True
        ).astype(jnp.float32),
        lax.psum_scatter(
            weight_sums[4].astype(jnp.bfloat16), "dp", scatter_dimension=2, tiled=True
        ).astype(jnp.float32),
        lax.psum_scatter(
            weight_sums[5].astype(jnp.bfloat16), "dp", scatter_dimension=1, tiled=True
        ).astype(jnp.float32),
    )
    vector_sums = (
        lax.psum_scatter(vector_sums[0], ("dp", "tensor"), scatter_dimension=1, tiled=True),
        lax.psum_scatter(vector_sums[1], ("dp", "tensor"), scatter_dimension=1, tiled=True),
        lax.psum_scatter(vector_sums[2], ("dp", "tensor"), scatter_dimension=0, tiled=True),
        lax.psum_scatter(vector_sums[3], ("dp", "tensor"), scatter_dimension=0, tiled=True),
    )
    states_all = jnp.stack(sent_rows)
    hidden_states = lax.dynamic_slice_in_dim(states_all, section_index, micro_count, 0)[None]
    grads_all = jnp.stack(entry_grads[::-1])
    input_grads = lax.dynamic_slice_in_dim(grads_all, section_index, micro_count, 0)[None]
    return (
        hidden_states,
        input_grads,
        vector_sums[0][None],
        vector_sums[1][None],
        weight_sums[0][None],
        weight_sums[4][None],
        weight_sums[1][None],
        vector_sums[2][None],
        weight_sums[2][None],
        weight_sums[5][None],
        weight_sums[3][None],
        vector_sums[3][None],
    )


def solution(mesh):
    return jax.shard_map(
        local,
        mesh=mesh,
        in_specs=(
            P(None, ("dp", "tensor"), None),
            P(None, ("dp", "tensor"), None),
            P(None, "dp"),
            P(None, "dp"),
            P("section", None, ("dp", "tensor")),
            P("section", None, ("dp", "tensor")),
            P("section", "dp", None, "tensor"),
            P("section", None, "tensor", "dp"),
            P("section", "tensor", "dp"),
            P("section", ("dp", "tensor")),
            P("section", "dp", "tensor"),
            P("section", "tensor", "dp"),
            P("section", "tensor", "dp"),
            P("section", ("dp", "tensor")),
        ),
        out_specs=(
            P("section", None, ("dp", "tensor"), None),
            P("section", None, ("dp", "tensor"), None),
            P("section", None, ("dp", "tensor")),
            P("section", None, ("dp", "tensor")),
            P("section", "dp", None, "tensor"),
            P("section", None, "tensor", "dp"),
            P("section", "tensor", "dp"),
            P("section", ("dp", "tensor")),
            P("section", "dp", "tensor"),
            P("section", "tensor", "dp"),
            P("section", "tensor", "dp"),
            P("section", ("dp", "tensor")),
        ),
        check_vma=False,
    )
```

profile of v0, /device:TPU:1, one launch (start us, length us, event | category | flops | bytes accessed | tf_op | source)
XLA Modules:
  0.0 1712.0 jit_solution(12008848138817256211)
XLA Ops:
  13.9 83.4 %all-gather.6 = bf16[1,8,128]{1,0,2:T(2,128)(2,1)S(1)} all-gather(bf16[1,8,4]{1,0,2:T(2,128)(2,1)S(1)} %copy.133), channel_id=8, replica_groups=mesh['section'=2,'dp'=32,'tensor'=2] {'dp'}, dimensions={2}, use_global_device_ids=true | all-gather | bytes 2112 | tf_op jit(solution)/shard_map/all_gather | solution.py:282
  97.3 73.8 %all-gather.3 = bf16[1,3,4,64]{2,1,0,3:T(4,128)(2,1)S(1)} all-gather(bf16[1,3,4,2]{2,1,0,3:T(4,128)(2,1)S(1)} %copy.129), channel_id=5, replica_groups=mesh['section'=2,'dp'=32,'tensor'=2] {'dp'}, dimensions={3}, use_global_device_ids=true | all-gather | bytes 1584 | tf_op jit(solution)/shard_map/all_gather | solution.py:281
  171.3 119.4 %all-gather.1 = bf16[1,2,512]{1,0,2:T(2,128)(2,1)S(1)} all-gather(bf16[1,2,8]{1,0,2:T(2,128)(2,1)S(1)} %copy.127), channel_id=3, replica_groups=mesh['section'=2,'dp'=32,'tensor'=2] {'dp','tensor'}, dimensions={2}, use_global_device_ids=true | all-gather | bytes 2080 | tf_op jit(solution)/shard_map/all_gather | solution.py:286
  293.8 89.2 %all-gather = bf16[1,2,512]{1,0,2:T(2,128)(2,1)S(1)} all-gather(bf16[1,2,8]{1,0,2:T(2,128)(2,1)S(1)} %copy.126), channel_id=2, replica_groups=mesh['section'=2,'dp'=32,'tensor'=2] {'dp','tensor'}, dimensions={2}, use_global_device_ids=true | all-gather | bytes 2080 | tf_op jit(solution)/shard_map/all_gather | solution.py:285
  391.5 79.2 %all-gather.2 = bf16[1,512,3,256]{3,1,2,0:T(8,128)(2,1)S(1)} all-gather(bf16[1,16,3,256]{3,1,2,0:T(8,128)(2,1)S(1)} %copy-done.111), channel_id=4, replica_groups=mesh['section'=2,'dp'=32,'tensor'=2] {'dp'}, dimensions={1}, use_global_device_ids=true | all-gather | bytes 811008 | tf_op jit(solution)/shard_map/all_gather | solution.py:277
  480.4 75.0 %all-gather.4 = bf16[1,256,512]{1,2,0:T(8,128)(2,1)S(1)} all-gather(bf16[1,256,16]{1,2,0:T(8,128)(2,1)S(1)} %copy-done.136), channel_id=6, replica_groups=mesh['section'=2,'dp'=32,'tensor'=2] {'dp'}, dimensions={2}, use_global_device_ids=true | all-gather | bytes 270336 | tf_op jit(solution)/shard_map/all_gather | solution.py:278
  555.9 7.8 multiply_convert_fusion.5
  563.7 3.3 convolution_add_fusion.5
  568.8 190.4 %all-reduce.8 = (bf16[512]{0:T(512)(128)(2,1)S(1)}, bf16[512]{0:T(512)(128)(2,1)S(1)}) all-reduce(bf16[512]{0:T(512)(128)(2,1)S(1)} %dynamic-update-slice.1, bf16[512]{0:T(512)(128)(2,1)S(1)} %dynamic-update-slice), channel_id=11, replica_groups=mesh['section'=2,'dp'=32,'tensor'=2] {'dp','tensor'}, use_global_device_ids=true, to_apply=%add.1 | all-reduce | flops 1024 | bytes 4096
  762.7 4.8 collective-permute-done
  768.7 3.5 all_gather.74
  786.8 6.5 multiply_convert_fusion.4
  799.5 4.5 reduce-scatter.20.cloned.1.call-done
  805.1 3.2 collective-permute-start.1
  815.8 3.3 all_gather.75
  841.7 7.2 multiply_convert_fusion.3
  853.8 3.8 fusion.52
  860.6 9.3 reduce-scatter.26.cloned.1.call-done
  876.0 8.8 reduce-scatter.22.cloned.1.call-done
  890.1 7.9 collective-permute-done.2
  903.5 3.7 convert_reduce_fusion.1
  910.3 4.0 multiply_reduce_fusion.1
  928.8 9.1 reduce-scatter.28.cloned.1.call-done
  945.6 8.1 collective-permute-done.3
  973.7 3.8 convert_reduce_fusion
  996.6 157.9 %all-reduce.9 = (bf16[3,4,64]{1,2,0:T(8,128)(2,1)S(1)}, bf16[8,128]{1,0:T(8,128)(2,1)S(1)}) all-reduce(bf16[3,4,64]{1,2,0:T(8,128)(2,1)S(1)} %copy.151, bf16[8,128]{1,0:T(8,128)(2,1)S(1)} %fusion.203), channel_id=24, replica_groups=mesh['section'=2,'dp'=32,'tensor'=2] {'dp'}, use_global_device_ids=true, to_apply=%region_54.55.clone | all-reduce | flops 1792 | bytes 7168
  1155.3 3.8 add_convert_fusion.1
  1161.2 147.6 %reduce-scatter.36.cloned.1.call-done = bf16[16,3,256]{2,0,1:T(8,128)(2,1)} async-done(((bf16[512,3,256]{2,0,1:T(8,128)(2,1)}), bf16[16,3,256]{2,0,1:T(8,128)(2,1)}) %reduce-scatter.36.cloned.1.call-update) | async-done | bytes 24592 | tf_op jit(solution)/shard_map/reduce_scatter | solution.py:346
  1310.1 32.5 %reduce-scatter.34.cloned.1.call-done = f32[256,512]{1,0:T(8,128)} async-done(((f32[512,512]{1,0:T(8,128)}), f32[256,512]{1,0:T(8,128)}) %reduce-scatter.34.cloned.1.call-update) | async-done | bytes 524304 | tf_op jit(solution)/shard_map/reduce_scatter | solution.py:224
  1342.6 14.9 reduce-scatter.32.cloned.1.call-done
  1361.1 325.1 %all-reduce.7 = (f32[2,512]{1,0:T(2,128)S(1)}, f32[2,512]{1,0:T(2,128)S(1)}, f32[512]{0:T(512)S(1)}) all-reduce(f32[2,512]{1,0:T(2,128)S(1)} %fusion.195, f32[2,512]{1,0:T(2,128)S(1)} %fusion.196, f32[512]{0:T(512)S(1)} %add_add_fusion.7), channel_id=21, replica_groups=mesh['section'=2,'dp'=32,'tensor'=2] {'dp','tensor'}, use_global_device_ids=true, to_apply=%region_42.43.clone | all-reduce | flops 2560 | bytes 20480
  1690.5 12.6 reduce-scatter.40.cloned.1.call-done
  (546 shorter events, 185.6 us)
Async XLA Ops:
  7.2 379.6 %copy-start.5 = (bf16[2,256,512]{2,1,0:T(8,128)(2,1)S(1)}, bf16[2,256,512]{2,1,0:T(8,128)(2,1)}, u32[]{:S(2)}) copy-start(bf16[2,256,512]{2,1,0:T(8,128)(2,1)} %param.14) | copy-start | bytes 1572868
  7.2 378.8 %copy-start.126 = (s32[2,512]{1,0:T(2,128)S(1)}, s32[2,512]{1,0:T(2,128)}, u32[]{:S(2)}) copy-start(s32[2,512]{1,0:T(2,128)} %param.17) | copy-start | bytes 12292
  7.2 378.8 %copy-start.125 = (s32[2,512]{1,0:T(2,128)S(1)}, s32[2,512]{1,0:T(2,128)}, u32[]{:S(2)}) copy-start(s32[2,512]{1,0:T(2,128)} %param.16) | copy-start | bytes 12292
  7.2 548.6 %all-gather.13.cloned.1.call-start = ((), (), s32[]{:S(2)}) async-start(), calls=%async_computation.26 | async-start | bytes 1081344 | tf_op jit(solution)/shard_map/all_gather | solution.py:279
  7.9 555.7 %all-gather.15.cloned.1.call-start = ((), (), s32[]{:S(2)}) async-start(), calls=%async_computation.27 | async-start | bytes 1081344 | tf_op jit(solution)/shard_map/all_gather | solution.py:280
  8.7 750.5 %reduce-scatter.18.cloned.1.call-start = ((), (), s32[]{:S(2)}) async-start(), calls=%async_computation.13 | async-start | bytes 1572864 | tf_op jit(solution)/shard_map/reduce_scatter | solution.py:174
  9.9 377.2 %copy-start.87 = (f32[256]{0:T(256)}, f32[256]{0:T(256)S(1)}, u32[]{:S(2)}) copy-start(f32[256]{0:T(256)S(1)} %broadcast_multiply_fusion.2) | copy-start | bytes 3076
  11.0 378.3 %copy-start.113 = (f32[256]{0:T(256)}, f32[256]{0:T(256)S(1)}, u32[]{:S(2)}) copy-start(f32[256]{0:T(256)S(1)} %fusion.206) | copy-start | bytes 3076
  171.3 299.7 %copy-start.143 = (f32[768]{0:T(1024)}, f32[768]{0:T(1024)S(1)}, u32[]{:S(2)}) copy-start(f32[768]{0:T(1024)S(1)} %reshape.759) | copy-start | bytes 9220
  566.9 237.0 %reduce-scatter.20.cloned.1.call-start = ((), (), s32[]{:S(2)}) async-start(), calls=%async_computation.14 | async-start | bytes 1572864 | tf_op jit(solution)/shard_map/reduce_scatter | solution.py:174
  760.4 7.0 collective-permute-start
  796.1 64.5 %reduce-scatter.24.cloned.1.call-start = ((), (), s32[]{:S(2)}) async-start(), calls=%async_computation.16 | async-start | bytes 1572864 | tf_op jit(solution)/shard_map/reduce_scatter | solution.py:223
  805.1 8.7 collective-permute-start.1
  841.4 28.4 %reduce-scatter.26.cloned.1.call-start = ((), (), s32[]{:S(2)}) async-start(), calls=%async_computation.17 | async-start | bytes 1572864 | tf_op jit(solution)/shard_map/reduce_scatter | solution.py:224
  853.7 31.1 %reduce-scatter.22.cloned.1.call-start = ((), (), s32[]{:S(2)}) async-start(), calls=%async_computation.15 | async-start | bytes 1572864 | tf_op jit(solution)/shard_map/reduce_scatter | solution.py:174
  860.5 68.2 %reduce-scatter.30.cloned.1.call-start = ((), (), s32[]{:S(2)}) async-start(), calls=%async_computation.19 | async-start | bytes 1572864 | tf_op jit(solution)/shard_map/reduce_scatter | solution.py:224
  887.8 10.2 collective-permute-start.2
  910.0 27.8 %reduce-scatter.28.cloned.1.call-start = ((), (), s32[]{:S(2)}) async-start(), calls=%async_computation.18 | async-start | bytes 1572864 | tf_op jit(solution)/shard_map/reduce_scatter | solution.py:223
  921.6 238.3 %reduce-scatter.38.cloned.1.call-start = ((), (), s32[]{:S(2)}) async-start(), calls=%async_computation.23 | async-start | bytes 270336 | tf_op jit(solution)/shard_map/reduce_scatter | solution.py:349
  943.7 10.0 collective-permute-start.3
  966.6 342.1 %reduce-scatter.36.cloned.1.call-start = ((), (), s32[]{:S(2)}) async-start(), calls=%async_computation.22 | async-start | bytes 811008 | tf_op jit(solution)/shard_map/reduce_scatter | solution.py:346
  973.6 369.0 %reduce-scatter.34.cloned.1.call-start = ((), (), s32[]{:S(2)}) async-start(), calls=%async_computation.21 | async-start | bytes 1572864 | tf_op jit(solution)/shard_map/reduce_scatter | solution.py:224
  980.4 377.2 %reduce-scatter.32.cloned.1.call-start = ((), (), s32[]{:S(2)}) async-start(), calls=%async_computation.20 | async-start | bytes 1572864 | tf_op jit(solution)/shard_map/reduce_scatter | solution.py:223
  982.0 707.0 %reduce-scatter.42.cloned.1.call-start = ((), (), s32[]{:S(2)}) async-start(), calls=%async_computation.25 | async-start | bytes 1081344 | tf_op jit(solution)/shard_map/reduce_scatter | solution.py:355
  987.4 715.7 %reduce-scatter.40.cloned.1.call-start = ((), (), s32[]{:S(2)}) async-start(), calls=%async_computation.24 | async-start | bytes 1081344 | tf_op jit(solution)/shard_map/reduce_scatter | solution.py:352
  1155.3 202.2 %copy-start.88 = (f32[256]{0:T(256)S(1)}, f32[256]{0:T(256)}, u32[]{:S(2)}) copy-start(f32[256]{0:T(256)} %copy-done.87) | copy-start | bytes 3076
  1159.1 201.9 %copy-start.137 = (f32[512]{0:T(512)S(1)}, f32[512]{0:T(512)}, u32[]{:S(2)}) copy-start(f32[512]{0:T(512)} %get-tuple-element.133) | copy-start | bytes 6148
  1159.2 528.3 %copy-start.35 = (bf16[256,512]{1,0:T(8,128)(2,1)S(1)}, bf16[256,512]{1,0:T(8,128)(2,1)}, u32[]{:S(2)}) copy-start(bf16[256,512]{1,0:T(8,128)(2,1)} %copy-done.34) | copy-start | bytes 786436
  1342.6 344.9 %copy-start.23 = (f32[256,512]{1,0:T(8,128)S(1)}, f32[256,512]{1,0:T(8,128)}, u32[]{:S(2)}) copy-start(f32[256,512]{1,0:T(8,128)} %reduce-scatter.34.cloned.1.call-done) | copy-start | bytes 1572868
  1357.5 330.0 %copy-start.24 = (f32[256,512]{1,0:T(8,128)S(1)}, f32[256,512]{1,0:T(8,128)}, u32[]{:S(2)}) copy-start(f32[256,512]{1,0:T(8,128)} %reduce-scatter.32.cloned.1.call-done) | copy-start | bytes 1572868
  1359.1 328.8 %copy-start.46 = (f32[256,512]{1,0:T(8,128)S(1)}, f32[256,512]{1,0:T(8,128)}, u32[]{:S(2)}) copy-start(f32[256,512]{1,0:T(8,128)} %get-tuple-element.223) | copy-start | bytes 1572868
  1359.1 328.8 %copy-start.47 = (f32[256,512]{1,0:T(8,128)S(1)}, f32[256,512]{1,0:T(8,128)}, u32[]{:S(2)}) copy-start(f32[256,512]{1,0:T(8,128)} %get-tuple-element.219) | copy-start | bytes 1572868
  (148 other events, 3403.6 us)
Sparse Core Ops, SparseCore 0:
  11.0 68.0 all-gather.12
  82.1 63.3 all-gather.14
  567.1 34.7 reduce-scatter.17
  796.2 7.6 reduce-scatter.19
  841.5 13.3 reduce-scatter.23
  857.2 12.5 reduce-scatter.25
  872.2 12.5 reduce-scatter.21
  910.1 12.7 reduce-scatter.29
  925.2 12.5 reduce-scatter.27
  966.7 159.4 reduce-scatter.37
  1128.6 180.0 reduce-scatter.35
  1311.1 31.5 reduce-scatter.33
  1345.0 12.5 reduce-scatter.31
  1359.9 161.9 reduce-scatter.41
  1524.0 179.0 reduce-scatter.39
where the time goes:
time: 1740 us; the launch traced here: 1710 us
  blocking collectives  1220 us (70%)
  waiting for transfers between devices  264 us (15%)
  matrix products  108 us (6%)
  other arithmetic  53.7 us (3%)
  local copies, waits for them, and re-layouts  40.7 us (2%)
  between operations  19.2 us (1%)
    unnamed x3, blocking collectives  673 us
    reduce_scatter x1, waiting for transfers between devices, local(): lax.psum_scatter(weight_sums[0].astype(jnp.bfloat16), 'dp', scatter_dimen...  148 us
    all_gather x1, blocking collectives, local(): lax.all_gather(norm_shifts[0], ('dp', 'tensor'), axis=1, tiled=True)  119 us
    all_gather x1, blocking collectives, local(): lax.all_gather(norm_gains[0], ('dp', 'tensor'), axis=1, tiled=True)  89.2 us
    all_gather x1, blocking collectives, local(): lax.all_gather(pieces[5], 'dp', axis=1, tiled=True)  83.4 us
    all_gather x1, blocking collectives, local(): lax.all_gather(pieces[0], 'dp', axis=0, tiled=True)  79.2 us
    all_gather x1, blocking collectives, local(): lax.all_gather(pieces[1], 'dp', axis=1, tiled=True)  75 us
    all_gather x1, blocking collectives, local(): lax.all_gather(pieces[4], 'dp', axis=2, tiled=True)  73.8 us
  transfers between devices with their start and end apart: 19, of which 12 were waited for; matrix products, arithmetic and copies ran while one was open for 7% of the time, Pallas kernels for 0%

commit v1 on v0

v1 whole, which is shorter than its diff:
```python
import jax
import jax.numpy as jnp
import numpy as np
from jax import lax
from jax.experimental import pallas as pl
from jax.experimental.pallas import tpu as pltpu
from jax.sharding import PartitionSpec as P

MESH = pl.DeviceIdType.MESH
BF = jnp.bfloat16
F32 = jnp.float32
HD = 64
ROT = 16
LEN = 512
D = 512
OWN = 256
HEADS = 4
EPSILON = 1e-05
MASKED = -1e30

COLS = 3200
IN, OUT, EXP, SHR, VEC = 0, 768, 1024, 2048, 3072
PARTS = ((0, 1024), (1024, 1024), (2048, 1152))
ORDERS = (("y", "z", "x"), ("z", "x", "y"), ("x", "y", "z"))
HALF = 512

V_IN, V_EXP, V_OUTB, V_SHRB, V_G0, V_G1, V_B0, V_B1, V_ALL = 0, 768, 1792, 2304, 2816, 3328, 3840, 4352, 4864


def where_am_i():
    s = lax.axis_index("section"); d = lax.axis_index("dp")
    return {"x": d % 4, "z": (d // 4) % 4, "y": (d // 16) * 2 + s}


def chip_id(c):
    return {"section": c["y"] % 2, "dp": (c["y"] // 2) * 16 + c["z"] * 4 + c["x"]}


def moved(c, axis, by):
    return {**c, axis: (c[axis] + by) % 4}


def slots(c, free, fixed_axis_val=None):
    full = slice(None)
    y = c["y"]
    return ((full, full) if "y" in free else (y % 2, y // 2)) + (
        full if "z" in free else c["z"], full if "x" in free else c["x"])


def region(ref, c, free, lo, width):
    return ref.at[slots(c, free) + (slice(None), pl.ds(lo, width))]


def greet(c):
    barrier = pltpu.get_barrier_semaphore()
    for axis in "xyz":
        for by in (1, -1):
            pl.semaphore_signal(barrier, inc=1, device_id=chip_id(moved(c, axis, by)), device_id_type=MESH)
    pl.semaphore_signal(barrier, inc=1, device_id={"tensor": 1 - lax.axis_index("tensor")}, device_id_type=MESH)
    pl.semaphore_wait(barrier, 7)


def push(src, dst, send, recv, target):
    return pltpu.make_async_remote_copy(src_ref=src, dst_ref=dst, send_sem=send, recv_sem=recv, device_id=target, device_id_type=MESH)


def gather(held, c, send, recv):
    for stage in range(3):
        first = []
        for p, (lo, width) in enumerate(PARTS):
            axis = ORDERS[p][stage]; done = ORDERS[p][:stage]
            own = region(held, c, done, lo, width)
            pair = []
            for k, by in enumerate((1, -1)):
                cp = push(own, own, send.at[p, stage, k], recv.at[p, stage, k], chip_id(moved(c, axis, by)))
                cp.start(); pair.append(cp)
            first.append(pair)
        second = []
        for p, (lo, width) in enumerate(PARTS):
            axis = ORDERS[p][stage]; done = ORDERS[p][:stage]
            pair = []
            for k, by in enumerate((1, -1)):
                src = moved(c, axis, -by)
                got = region(held, src, done, lo, width)
                push(got, got, send.at[p, stage, k], recv.at[p, stage, k], chip_id(src)).wait_recv()
                sub = (lo, HALF) if k == 0 else (lo + HALF, width - HALF)
                part = region(held, src, done, *sub)
                cp = push(part, part, send.at[p, stage, 2 + k], recv.at[p, stage, 2 + k], chip_id(moved(c, axis, by)))
                cp.start(); pair.append(cp)
            second.append(pair)
        for p, (lo, width) in enumerate(PARTS):
            axis = ORDERS[p][stage]; done = ORDERS[p][:stage]
            far = moved(c, axis, 2)
            for k in range(2):
                sub = (lo, HALF) if k == 0 else (lo + HALF, width - HALF)
                part = region(held, far, done, *sub)
                push(part, part, send.at[p, stage, 2 + k], recv.at[p, stage, 2 + k], chip_id(far)).wait_recv()
        for pair in first + second:
            for cp in pair:
                cp.wait_send()


def reduce_shapes(p, stage):
    lo, width = PARTS[p]
    order = ORDERS[p][::-1]
    pend = order[stage + 1:]
    lead = ((2, 2) if "y" in pend else ()) + ((4,) if "z" in pend else ()) + ((4,) if "x" in pend else ())
    return [lead + (16, HALF), lead + (16, width - HALF), lead + (16, width), lead + (16, width)]


def reduce_scratch():
    return [pltpu.VMEM(s, BF) for p in range(3) for st in range(3) for s in reduce_shapes(p, st)]


def accumulate(total, c, free, lo, width, others):
    dims = []
    for ax in "yzx":
        if ax in free:
            dims.append((ax, 4))
    n = 4 ** len(dims)

    def body(i, _):
        cc = dict(c); rest = i; lead = {}
        for ax, size in reversed(dims):
            cc[ax] = rest % 4; rest = rest // 4
        at = (cc["y"] % 2, cc["y"] // 2, cc["z"], cc["x"], slice(None), pl.ds(lo, width))
        oat = ()
        if "y" in free: oat += (cc["y"] % 2, cc["y"] // 2)
        if "z" in free: oat += (cc["z"],)
        if "x" in free: oat += (cc["x"],)
        v = total[at].astype(F32)
        for o in others:
            v = v + o[oat].astype(F32)
        total[at] = v.astype(BF)
        return 0
    if n == 1:
        body(0, 0)
    else:
        lax.fori_loop(0, n, body, 0)


def reduce(total, c, bufs, send, recv):
    buf = lambda p, st, k: bufs[(p * 3 + st) * 4 + k]
    for stage in range(3):
        first, second = [], []
        for p, (lo, width) in enumerate(PARTS):
            order = ORDERS[p][::-1]; axis = order[stage]; pend = order[stage + 1:]
            far = moved(c, axis, 2)
            for k, by in enumerate((1, -1)):
                sub = (lo, HALF) if k == 0 else (lo + HALF, width - HALF)
                cp = push(region(total, far, pend, *sub), buf(p, stage, k), send.at[p, stage, k], recv.at[p, stage, k], chip_id(moved(c, axis, by)))
                cp.start(); first.append(cp)
        for p, (lo, width) in enumerate(PARTS):
            order = ORDERS[p][::-1]; axis = order[stage]; pend = order[stage + 1:]
            for k, by in enumerate((1, -1)):
                sub = (lo, HALF) if k == 0 else (lo + HALF, width - HALF)
                first[2 * p + k].wait_recv()
                to = moved(c, axis, by)
                accumulate(total, to, pend, *sub, [buf(p, stage, k)])
                cp = push(region(total, to, pend, lo, width), buf(p, stage, 2 + k), send.at[p, stage, 2 + k], recv.at[p, stage, 2 + k], chip_id(to))
                cp.start(); second.append(cp)
        for p, (lo, width) in enumerate(PARTS):
            order = ORDERS[p][::-1]; axis = order[stage]; pend = order[stage + 1:]
            for k in range(2):
                second[2 * p + k].wait_recv()
            accumulate(total, c, pend, lo, width, [buf(p, stage, 2), buf(p, stage, 3)])
        for cp in first + second:
            cp.wait_send()


def dot(a, b):
    return jnp.dot(a, b, preferred_element_type=F32)


def dot_nt(a, b):
    return lax.dot_general(a, b, (((1,), (1,)), ((), ())), preferred_element_type=F32)


def weight(held, layer, lo, width):
    return held[layer, :, :, :, :, lo : lo + width].reshape(D, width)


def keep_grad(total, layer, lo, value):
    width = value.shape[-1]
    total[layer, :, :, :, :, lo : lo + width] = value.astype(BF).reshape(2, 4, 4, 16, width)


def vector_maps():
    at = lax.broadcasted_iota(jnp.int32, (1, V_ALL), 1)
    exp_at = at - V_EXP
    wide = at - V_OUTB
    wide_at = wide & 511
    is_in, is_exp = at < V_EXP, at < V_OUTB
    owner = jnp.where(is_in, (at & 63) >> 1, jnp.where(is_exp, (exp_at & 127) >> 2, wide_at >> 4))
    lane = jnp.where(
        is_in,
        ((at >> 6) << 1) + (at & 1),
        jnp.where(is_exp, 24 + ((exp_at >> 7) << 2) + (exp_at & 3), 56 + ((wide >> 9) << 3) + (wide_at & 7)),
    )
    core = (wide_at >> 3) & 1
    return owner, lane, core, is_exp


def decode_vectors(held, layer, me, table):
    owner, lane, core, is_exp = vector_maps()
    owners = lax.broadcasted_iota(jnp.int32, (32, V_ALL), 0)
    block = held[layer, :, :, :, :, VEC:COLS].reshape(32, 16, 128).astype(F32)
    result = jnp.zeros((1, V_ALL), F32)
    for row in range(2):
        spread = dot(block[:, row, :].astype(BF), table[...])
        wanted = jnp.where(jnp.where(is_exp, me, core) == row, owner, -1)
        result = result + jnp.sum(jnp.where(owners == wanted, spread, 0.0), axis=0, keepdims=True)
    return result


def encode_vectors(total, layer, me, table, vectors):
    owner, lane, core, is_exp = vector_maps()
    at = lax.broadcasted_iota(jnp.int32, (1, V_ALL), 1)
    owners = lax.broadcasted_iota(jnp.int32, (32, V_ALL), 0)
    rows = []
    for row in range(2):
        source = jnp.where(at < V_OUTB, me, jnp.where((at >= V_G0) | (core == me), core, 2))
        wanted = jnp.where(source == row, owner, -1)
        chosen = jnp.where(owners == wanted, vectors, 0.0).astype(BF)
        rows.append(dot_nt(chosen, table[...]))
    row_at = lax.broadcasted_iota(jnp.int32, (32, 16, 128), 1)
    block = jnp.where(row_at == 0, rows[0][:, None, :], jnp.where(row_at == 1, rows[1][:, None, :], 0.0))
    total[layer, :, :, :, :, VEC:COLS] = block.astype(BF).reshape(2, 4, 4, 16, 128)


def rolled(values, by):
    return pltpu.roll(values, by % values.shape[-1], 1)


def turned(values, cosine, sine_front, sine_back):
    return values * cosine + rolled(values, -(ROT // 2)) * sine_front + rolled(values, ROT // 2) * sine_back


def rows_of(i):
    return pl.ds(pl.multiple_of(i * OWN, OWN), OWN)


def forward(layer, r):
    held, vec = r.held, r.vec

    def project(i, carry):
        rows = rows_of(i)
        x = r.x[layer, rows, :].astype(F32)
        middle = jnp.mean(x, axis=-1, keepdims=True)
        center = x - middle
        scale = lax.rsqrt(jnp.mean(center * center, axis=-1, keepdims=True) + EPSILON)
        normal = center * scale
        r.moments[layer, 0, rows, :] = jnp.broadcast_to(middle, (OWN, 128))
        r.moments[layer, 1, rows, :] = jnp.broadcast_to(scale, (OWN, 128))
        first = (normal * vec[layer, :, V_G0:V_G1] + vec[layer, :, V_B0:V_B1]).astype(BF)
        second = (normal * vec[layer, :, V_G1:V_B0] + vec[layer, :, V_B1:V_ALL]).astype(BF)
        r.first_t[layer, :, rows] = first.T
        r.second_t[layer, :, rows] = second.T
        joint = dot(first, weight(held, layer, IN, 768)) + vec[layer, :, V_IN:V_EXP]
        cosine, front, back = [jnp.concatenate([r.angles[k, rows, :]] * 2, axis=1) for k in range(3)]
        query = turned(joint[:, :256], cosine, front, back).astype(BF) * BF(HD**-0.5)
        key = turned(joint[:, 256:512], cosine, front, back).astype(BF)
        value = joint[:, 512:].astype(BF)
        for k, part in enumerate((query, key, value)):
            part_t = part.T
            for h in range(HEADS):
                r.qkv[layer, k, h, rows, :] = part[:, h * HD : (h + 1) * HD]
                r.qkv_t[layer, k, h, :, rows] = part_t[h * HD : (h + 1) * HD]
        before = dot(second, weight(held, layer, EXP, 1024)) + vec[layer, :, V_EXP:V_OUTB]
        chance = 0.5 * (1.0 + lax.erf(before * (0.5**0.5)))
        r.hidden[layer, rows, :] = (before * chance).astype(BF)
        slope = chance + before * jnp.exp(-0.5 * before * before) * ((2.0 * np.pi) ** -0.5)
        r.slope[layer, rows, :] = slope.astype(BF)
        return carry

    lax.fori_loop(0, 2, project, 0)

    def attend(h, carry):
        for b in range(2):
            keys = (b + 1) * OWN
            cols = slice(b * OWN, keys)
            scores = dot(r.qkv[layer, 1, h, :keys, :], r.qkv_t[layer, 0, h, :, cols]) + r.mask[:keys, cols]
            powers = jnp.exp(scores - jnp.max(scores, axis=0, keepdims=True))
            shares = (powers * (1.0 / jnp.sum(powers, axis=0, keepdims=True))).astype(BF)
            r.shares[layer, h, :keys, cols] = shares
            r.mixed_t[layer, h, :, cols] = dot(r.qkv_t[layer, 2, h, :, :keys], shares)
        return carry

    lax.fori_loop(0, HEADS, attend, 0)
    r.mixed[layer] = r.mixed_t[layer].reshape(HEADS * HD, LEN).T.astype(BF)

    def close(i, carry):
        rows = rows_of(i)
        branch = dot_nt(r.mixed[layer, rows, :], weight(held, layer, OUT, 256))
        branch = branch + dot_nt(r.hidden[layer, rows, :], weight(held, layer, SHR, 1024))
        r.away[layer, rows, :] = branch.astype(BF)
        return carry

    lax.fori_loop(0, 2, close, 0)


def backward(layer, r):
    held, total, vec = r.held, r.total, r.vec

    def enter(i, carry):
        rows = rows_of(i)
        grad = r.grad[layer, rows, :]
        low = grad.astype(BF)
        r.grad_t[:, rows] = low.T
        mixed_grad = dot(low, weight(held, layer, OUT, 256)).astype(BF)
        mixed_grad_t = mixed_grad.T
        for h in range(HEADS):
            r.mixed_grad[h, rows, :] = mixed_grad[:, h * HD : (h + 1) * HD]
            r.mixed_grad_t[h, :, rows] = mixed_grad_t[h * HD : (h + 1) * HD]
        before = (dot(low, weight(held, layer, SHR, 1024)) * r.slope[layer, rows, :].astype(F32)).astype(BF)
        r.before_grad[rows, :] = before
        r.second_grad[rows, :] = dot_nt(before, weight(held, layer, EXP, 1024))
        return carry + jnp.sum(grad, axis=0, keepdims=True)

    out_sum = lax.fori_loop(0, 2, enter, jnp.zeros((1, D), F32))
    keep_grad(total, layer, OUT, dot(r.grad_t[...], r.mixed[layer]))
    for lo in range(0, 1024, 512):
        keep_grad(total, layer, SHR + lo, dot(r.grad_t[...], r.hidden[layer, :, lo : lo + 512]))
        keep_grad(total, layer, EXP + lo, dot(r.second_t[layer], r.before_grad[:, lo : lo + 512]))

    def attend(h, carry):
        key_parts, value_parts = [], []
        for b in range(2):
            keys = (b + 1) * OWN
            cols = slice(b * OWN, keys)
            shares = r.shares[layer, h, :keys, cols]
            out_t = r.mixed_grad_t[h, :, cols]
            delta = jnp.sum(out_t.astype(F32) * r.mixed_t[layer, h, :, cols], axis=0, keepdims=True)
            share_grad = dot(r.qkv[layer, 2, h, :keys, :], out_t)
            score_grad = (shares.astype(F32) * (share_grad - delta)).astype(BF)
            r.query_grad_t[h, :, cols] = dot(r.qkv_t[layer, 1, h, :, :keys], score_grad) * (HD**-0.5)
            key_parts.append(dot(score_grad, r.qkv[layer, 0, h, cols, :]))
            value_parts.append(dot(shares, r.mixed_grad[h, cols, :]))
        for k, parts in enumerate((key_parts, value_parts)):
            r.pair_grad[k, h, :OWN, :] = parts[0] + parts[1][:OWN]
            r.pair_grad[k, h, OWN:, :] = parts[1][OWN:]
        return carry

    lax.fori_loop(0, HEADS, attend, 0)

    def join(i, carry):
        rows = rows_of(i)
        cosine, front, back = [jnp.concatenate([r.angles[k, rows, :]] * 2, axis=1) for k in range(3)]
        query = r.query_grad_t[:, :, rows].reshape(HEADS * HD, OWN).T
        key = jnp.concatenate([r.pair_grad[0, h, rows, :] for h in range(HEADS)], axis=1)
        value = jnp.concatenate([r.pair_grad[1, h, rows, :] for h in range(HEADS)], axis=1)
        query = turned(query, cosine, -front, -back)
        key = turned(key, cosine, -front, -back)
        joint = jnp.concatenate([query, key, value], axis=1).astype(BF)
        r.joint_grad[rows, :] = joint
        first_grad = dot_nt(joint, weight(held, layer, IN, 768))
        second_grad = r.second_grad[rows, :]
        middle, scale = [jnp.concatenate([r.moments[layer, k, rows, :]] * 4, axis=1) for k in range(2)]
        normal = (r.x[layer, rows, :].astype(F32) - middle) * scale
        scaled = first_grad * vec[layer, :, V_G0:V_G1] + second_grad * vec[layer, :, V_G1:V_B0]
        passed = scaled - jnp.mean(scaled, axis=-1, keepdims=True)
        passed = passed - normal * jnp.mean(scaled * normal, axis=-1, keepdims=True)
        r.away[3 - layer, rows, :] = (passed * scale).astype(BF)
        sums = [joint.astype(F32), r.before_grad[rows, :].astype(F32), first_grad * normal, second_grad * normal, first_grad, second_grad]
        return tuple(c + jnp.sum(v, axis=0, keepdims=True) for c, v in zip(carry, sums))

    widths = (768, 1024, D, D, D, D)
    sums = lax.fori_loop(0, 2, join, tuple(jnp.zeros((1, w), F32) for w in widths))
    keep_grad(total, layer, IN, dot(r.first_t[layer], r.joint_grad[...]))
    vectors = jnp.concatenate([sums[0], sums[1], out_sum, out_sum, *sums[2:]], axis=1)
    encode_vectors(total, layer, r.me, r.table, vectors)


class Refs:
    pass


SCRATCH = dict(
    held=((2, 2, 4, 4, 16, COLS), BF),
    total=((2, 2, 4, 4, 16, COLS), BF),
    vec=((2, 1, V_ALL), F32),
    table=((128, V_ALL), BF),
    x=((2, LEN, D), BF),
    cot=((LEN, D), BF),
    grad=((2, LEN, D), F32),
    moments=((2, 2, LEN, 128), F32),
    first_t=((2, D, LEN), BF),
    second_t=((2, D, LEN), BF),
    qkv=((2, 3, HEADS, LEN, HD), BF),
    qkv_t=((2, 3, HEADS, HD, LEN), BF),
    shares=((2, HEADS, LEN, LEN), BF),
    mixed_t=((2, HEADS, HD, LEN), F32),
    mixed=((2, LEN, HEADS * HD), BF),
    hidden=((2, LEN, 1024), BF),
    slope=((2, LEN, 1024), BF),
    mask=((LEN, LEN), F32),
    away=((4, LEN, D), BF),
    come=((4, LEN, D), BF),
    grad_t=((D, LEN), BF),
    mixed_grad=((HEADS, LEN, HD), BF),
    mixed_grad_t=((HEADS, HD, LEN), BF),
    before_grad=((LEN, 1024), BF),
    second_grad=((LEN, D), F32),
    query_grad_t=((HEADS, HD, LEN), F32),
    pair_grad=((2, HEADS, LEN, HD), F32),
    joint_grad=((LEN, 768), BF),
    states=((2, OWN, D), BF),
    grads=((2, OWN, D), F32),
    grads_low=((2, OWN, D), BF),
    states_in=((OWN, D), BF),
    grads_in=((OWN, D), BF),
    small_in=((16, 128), BF),
    small_out=((16, 128), F32),
    small_back=((16, 128), F32),
)


def kernel(pack, x_in, cot_in, angles, seg_row, seg_col, states_out, grads_out, weights_out, vectors_out, *scratch):
    r = Refs()
    names = list(SCRATCH)
    for name, ref in zip(names, scratch):
        setattr(r, name, ref)
    gather_send, gather_recv, reduce_send, reduce_recv, near_send, near_recv, own_sem = scratch[len(names) : len(names) + 7]
    bufs = scratch[len(names) + 7 :]
    r.angles = angles
    c = where_am_i()
    section = lax.axis_index("section")
    me = r.me = lax.axis_index("tensor")
    other = {"tensor": 1 - me}
    mine = rows_of(me)

    def near(k, src, dst):
        return push(src, dst, near_send.at[k], near_recv.at[k], other)

    greet(c)
    small = near(0, pack.at[:, pl.ds(VEC, 128)], r.small_in)
    small.start()
    pairs = [near(1, x_in.at[section], r.x.at[0, mine]), near(2, cot_in.at[section], r.cot.at[mine])]
    owns = [
        pltpu.make_async_copy(x_in.at[section], r.x.at[0, mine], own_sem.at[0]),
        pltpu.make_async_copy(cot_in.at[section], r.cot.at[mine], own_sem.at[1]),
    ]
    for copy in pairs + owns:
        copy.start()
    held = r.held
    held[slots(c, ()) + (slice(None), slice(0, VEC))] = pack[:, :VEC]
    small.wait()
    both = pack[:, VEC:].astype(F32) + r.small_in[...].astype(F32)
    held[slots(c, ()) + (slice(None), slice(VEC, COLS))] = both.astype(BF)
    gather(held, c, gather_send, gather_recv)
    _, lane, _, _ = vector_maps()
    r.table[...] = (lax.broadcasted_iota(jnp.int32, (128, V_ALL), 0) == lane).astype(F32).astype(BF)
    for layer in range(2):
        r.vec[layer] = decode_vectors(held, layer, me, r.table)
    key_at = lax.broadcasted_iota(jnp.int32, (LEN, LEN), 0)
    query_at = lax.broadcasted_iota(jnp.int32, (LEN, LEN), 1)
    r.mask[...] = jnp.where((key_at <= query_at) & (seg_col[...] == seg_row[...]), 0.0, MASKED)
    for copy in pairs + owns:
        copy.wait()

    def swap(k):
        copy = near(3 + k, r.away.at[k], r.come.at[k])
        copy.start()
        copy.wait()

    for layer in range(2):
        forward(layer, r)
        swap(layer)
        bias = r.vec[layer, :, V_OUTB:V_SHRB] + r.vec[layer, :, V_SHRB:V_G0]

        def finish(rows):
            both = r.away[layer, rows, :].astype(F32) + r.come[layer, rows, :].astype(F32)
            return (r.x[layer, rows, :].astype(F32) + both + bias).astype(BF)

        if layer == 0:
            for i in range(2):
                rows = slice(i * OWN, (i + 1) * OWN)
                r.x[1, rows, :] = finish(rows)
        r.states[layer] = finish(mine)
    sides = [push(r.states.at[1 - section], r.states_in, near_send.at[8], near_recv.at[8], {"section": 1 - section})]
    sides[0].start()
    r.grad[1] = r.cot[...].astype(F32)
    for layer in (1, 0):
        backward(layer, r)
        swap(3 - layer)

        def pass_on(rows):
            both = r.away[3 - layer, rows, :].astype(F32) + r.come[3 - layer, rows, :].astype(F32)
            return r.grad[layer, rows, :] + both

        if layer == 1:
            for i in range(2):
                rows = slice(i * OWN, (i + 1) * OWN)
                r.grad[0, rows, :] = pass_on(rows).astype(BF).astype(F32)
        last = pass_on(mine)
        r.grads[layer] = last
        r.grads_low[layer] = last.astype(BF)
    sides.append(push(r.grads_low.at[1 - section], r.grads_in, near_send.at[9], near_recv.at[9], {"section": 1 - section}))
    sides[1].start()
    reduce(r.total, c, bufs, reduce_send, reduce_recv)
    own = r.total[slots(c, ())].astype(F32)
    weights_out[...] = own[:, :VEC]
    r.small_out[...] = own[:, VEC:]
    last = near(7, r.small_out, r.small_back)
    last.start()
    for copy in sides:
        copy.wait()
    states_out[section] = r.states[section]
    states_out[1 - section] = r.states_in[...]
    grads_out[section] = r.grads[section]
    grads_out[1 - section] = r.grads_in[...].astype(F32)
    last.wait()
    row_at = lax.broadcasted_iota(jnp.int32, (16, 128), 0)
    summed = lax.broadcasted_iota(jnp.int32, (16, 128), 1) >= 72
    value = r.small_out[...] + jnp.where(summed, r.small_back[...], 0.0)
    vectors_out[...] = jnp.sum(jnp.where(row_at == me, value, 0.0), axis=0, keepdims=True)


def rotary_tables(places):
    lane = np.arange(128) % HD
    rates = jnp.asarray(np.where(lane < ROT, 10000.0 ** (-2.0 * (lane % (ROT // 2)) / ROT), 0.0), F32)
    angles = places.astype(F32)[:, None] * rates[None, :]
    sine = jnp.sin(angles)
    front = jnp.where(jnp.asarray(lane < ROT // 2), -sine, 0.0)
    back = jnp.where(jnp.asarray((lane >= ROT // 2) & (lane < ROT)), sine, 0.0)
    return jnp.stack([jnp.cos(angles), front, back])


def local(
    block_input,
    out_cotangent,
    segments,
    positions,
    norm_gains,
    norm_shifts,
    inward_weight,
    inward_bias,
    outward_weight,
    outward_bias,
    expand_weight,
    expand_bias,
    shrink_weight,
    shrink_bias,
):
    section = lax.axis_index("section")
    me = lax.axis_index("tensor")
    labels = lax.dynamic_index_in_dim(segments, section, 0, keepdims=False)
    places = lax.dynamic_index_in_dim(positions, section, 0, keepdims=False)
    small = jnp.concatenate(
        [
            inward_bias.reshape(-1),
            expand_bias.reshape(-1),
            outward_bias.reshape(-1),
            shrink_bias.reshape(-1),
            norm_gains.reshape(-1),
            norm_shifts.reshape(-1),
            jnp.zeros((24,), BF),
        ]
    )
    small = jnp.where(jnp.arange(16)[:, None] == me, small[None, :], BF(0))
    pack = jnp.concatenate(
        [inward_weight[0].reshape(16, 768), outward_weight[0].T, expand_weight[0], shrink_weight[0].T, small], axis=1
    )
    vmem = pl.BlockSpec(memory_space=pltpu.VMEM)
    anywhere = pl.BlockSpec(memory_space=pl.ANY)
    dma = pltpu.SemaphoreType.DMA
    states, grads, weights, vectors = pl.pallas_call(
        kernel,
        out_shape=(
            jax.ShapeDtypeStruct((2, OWN, D), BF),
            jax.ShapeDtypeStruct((2, OWN, D), F32),
            jax.ShapeDtypeStruct((16, VEC), F32),
            jax.ShapeDtypeStruct((1, 128), F32),
        ),
        in_specs=[vmem, anywhere, anywhere, vmem, vmem, vmem],
        out_specs=(vmem,) * 4,
        scratch_shapes=[pltpu.VMEM(shape, kind) for shape, kind in SCRATCH.values()]
        + [dma((3, 3, 4)), dma((3, 3, 4)), dma((3, 3, 4)), dma((3, 3, 4)), dma((10,)), dma((10,)), dma((2,))]
        + reduce_scratch(),
        compiler_params=pltpu.CompilerParams(collective_id=0, has_side_effects=True, vmem_limit_bytes=62 << 20),
    )(pack, block_input, out_cotangent, rotary_tables(places), labels[None, :], labels[:, None])
    vec = vectors[0]
    return (
        states[None],
        grads[None],
        vec[72:88].reshape(1, 2, 8),
        vec[88:104].reshape(1, 2, 8),
        weights[:, IN:OUT].reshape(1, 16, 3, 256),
        vec[0:24].reshape(1, 3, 4, 2),
        weights[:, OUT:EXP].T[None],
        vec[56:64].reshape(1, 8),
        weights[:, EXP:SHR][None],
        vec[24:56].reshape(1, 8, 4),
        weights[:, SHR:VEC].T[None],
        vec[64:72].reshape(1, 8),
    )


def solution(mesh):
    return jax.shard_map(
        local,
        mesh=mesh,
        in_specs=(
            P(None, ("dp", "tensor"), None),
            P(None, ("dp", "tensor"), None),
            P(None, "dp"),
            P(None, "dp"),
            P("section", None, ("dp", "tensor")),
            P("section", None, ("dp", "tensor")),
            P("section", "dp", None, "tensor"),
            P("section", None, "tensor", "dp"),
            P("section", "tensor", "dp"),
            P("section", ("dp", "tensor")),
            P("section", "dp", "tensor"),
            P("section", "tensor", "dp"),
            P("section", "tensor", "dp"),
            P("section", ("dp", "tensor")),
        ),
        out_specs=(
            P("section", None, ("dp", "tensor"), None),
            P("section", None, ("dp", "tensor"), None),
            P("section", None, ("dp", "tensor")),
            P("section", None, ("dp", "tensor")),
            P("section", "dp", None, "tensor"),
            P("section", None, "tensor", "dp"),
            P("section", "tensor", "dp"),
            P("section", ("dp", "tensor")),
            P("section", "dp", "tensor"),
            P("section", "tensor", "dp"),
            P("section", "tensor", "dp"),
            P("section", ("dp", "tensor")),
        ),
        check_vma=False,
    )
```

time: 1740 us -> 161 us (0.09); the launches traced: 1710 us -> 160 us
  blocking collectives: 1220 us -> 0 us
  waiting for transfers between devices: 264 us -> 0 us
  Pallas kernels: 0 us -> 140 us
  matrix products: 108 us -> 0 us
  other arithmetic: 53.7 us -> 2.03 us
  local copies, waits for them, and re-layouts: 40.7 us -> 17.6 us
  between operations: 19.2 us -> 0.88 us
    unnamed x3 -> x0, blocking collectives: 673 us -> none
    all_gather x15 -> x0, blocking collectives: 544 us -> none  [the longest x1 119 us: local(): lax.all_gather(norm_shifts[0], ('dp', 'tensor'), axis=1, tiled=True)]
    reduce_scatter x13 -> x0, waiting for transfers between devices: 239 us -> none  [the longest x1 148 us: local(): lax.psum_scatter(weight_sums[0].astype(jnp.bfloat16), 'dp', scatter_dimen...]
    pallas_call x0 -> x1, Pallas kernels: none -> 140 us  [local(): pl.pallas_call(kernel, out_shape=(jax.ShapeDtypeStruct((2, OWN, D), BF),...]
    dot_general x54 -> x0, matrix products: 108 us -> none  [the longest x12 23.7 us: outer_rows(): lax.dot_general(left, right, (((0,), (0,)), ((), ())), preferred_element_...]
    reduce_sum x21 -> x0, other arithmetic: 23.9 us -> none  [the longest x6 12.4 us: norm_rows(): return center * lax.rsqrt(spread + EPSILON) * gain + shift]
    ppermute x4 -> x0, waiting for transfers between devices: 22.9 us -> none  [passed_along(): return lax.ppermute(array, axis, pairs)]
  transfers between devices with their start and end apart: 19 -> 0, of which waited for: 12 -> 0; matrix products, arithmetic and copies ran while one was open for 7% -> 0% of each run, Pallas kernels for 0% -> 0%
where the time goes in v1:
time: 161 us; the launch traced here: 160 us
  Pallas kernels  140 us (87%)
  local copies, waits for them, and re-layouts  17.6 us (11%)
  other arithmetic  2.03 us (1%)
    pallas_call x1, Pallas kernels, local(): pl.pallas_call(kernel, out_shape=(jax.ShapeDtypeStruct((2, OWN, D), BF),...  140 us
    unnamed x49, local copies, waits for them, and re-layouts  7.68 us

profile of v1, /device:TPU:1, one launch (start us, length us, event | category | flops | bytes accessed | tf_op | source)
XLA Modules:
  0.0 160.2 jit_solution(7323946431335688961)
XLA Ops:
  0.7 0.6 copy-done.16
  1.3 0.1 reshape.265
  1.4 0.1 reshape.266
  1.5 0.1 copy.37
  1.6 0.1 reshape.262
  1.7 0.1 copy.36
  1.8 0.1 reshape.261
  1.9 0.1 concatenate.6
  2.0 0.5 copy-done.8
  2.6 0.7 copy-done.6
  3.4 0.8 copy-done.3
  4.1 0.1 constant_dynamic-update-slice_fusion.pack
  4.2 0.9 copy.38.seg_col
  5.1 1.0 multiply_cosine_fusion
  6.1 0.9 pad_maximum_fusion.angles
  7.1 139.7 %shard_map.256 = (bf16[2,256,512]{2,1,0:T(8,128)(2,1)}, f32[2,256,512]{2,1,0:T(8,128)}, f32[16,3072]{1,0:T(8,128)}, f32[1,128]{1,0:T(1,128)}) custom-call(bf16[16,3200]{1,0:T(8,128)(2,1)} %copy-done.1, bf16[2,256,512]{2,1,0:T(8,128)(2,1)} %x_in.1, bf16[2,256,512]{2,1,0:T(8,128)(2,1)} %cot_in.1, f32[3,512,128]{2,1,0:T(8,128)} %pad_maximum_fusion.angles, ...), custom_call_target="tpu_custom_call" | custom-call | tf_op jit(solution)/shard_map/pallas_call | solution.py:567
  146.8 0.8 slice_reduce_fusion
  147.6 0.6 slice_reduce_fusion.1
  148.2 0.8 slice_reduce_fusion.2
  149.0 0.6 reshape.268
  149.6 1.3 fusion.3
  150.9 0.6 reshape.267
  151.5 0.1 reshape.271
  151.6 0.7 copy.41
  152.2 0.1 reshape.270
  152.3 0.7 copy.40
  153.0 1.3 slice_bitcast_fusion.2
  154.3 0.8 slice.38
  155.1 1.5 slice_bitcast_fusion
  156.7 0.6 copy.39
  157.3 1.9 %copy.49 = bf16[1,2,256,512]{3,2,1,0:T(8,128)(2,1)} copy(bf16[1,2,256,512]{3,2,1,0:T(8,128)(2,1)} %bitcast.30) | data formatting | bytes 1048576
  159.2 1.0 copy.50
  (42 shorter events, 0.2 us)
Async XLA Ops:
  0.7 0.7 copy-start.16
  0.7 0.7 copy-start.17
  0.7 1.2 copy-start.11
  0.7 1.2 copy-start.12
  0.7 0.8 copy-start.10
  0.7 1.0 copy-start.7
  0.7 1.8 %copy-start.4 = (bf16[1,16,3,256]{3,1,2,0:T(8,128)(2,1)S(1)}, bf16[1,16,3,256]{3,1,2,0:T(8,128)(2,1)}, u32[]{:S(2)}) copy-start(bf16[1,16,3,256]{3,1,2,0:T(8,128)(2,1)} %param.23) | copy-start | bytes 73732
  1.8 0.7 copy-start.8
  1.8 0.7 copy-start.9
  2.5 1.7 %copy-start.5 = (s32[1,512]{1,0:T(1,128)}, s32[1,512]{1,0:T(1,128)S(1)}, u32[]{:S(2)}) copy-start(s32[1,512]{1,0:T(1,128)S(1)} %get-tuple-element.54.seg_row) | copy-start | bytes 6148
  2.6 0.7 copy-start.6
  2.6 0.8 copy-start.2
  3.3 0.8 copy-start.3
  4.2 0.9 copy-start.1
  4.2 0.9 copy-start.13
  4.2 0.9 copy-start.14
  4.2 0.9 copy-start.15
  146.8 12.4 %copy-start = (f32[2,256,512]{2,1,0:T(8,128)S(1)}, f32[2,256,512]{2,1,0:T(8,128)}, u32[]{:S(2)}) copy-start(f32[2,256,512]{2,1,0:T(8,128)} %get-tuple-element.17) | copy-start | bytes 3145732

commit v2 on v1

v2 whole, which is shorter than its diff:
```python
import jax
import jax.numpy as jnp
import numpy as np
from jax import lax
from jax.experimental import pallas as pl
from jax.experimental.pallas import tpu as pltpu
from jax.sharding import PartitionSpec as P

MESH = pl.DeviceIdType.MESH
BF = jnp.bfloat16
F32 = jnp.float32
HD = 64
ROT = 16
LEN = 512
D = 512
OWN = 256
HEADS = 4
EPSILON = 1e-05
MASKED = -1e30

COLS = 3200
VEC, IN, OUT, EXP, SHR = 0, 128, 896, 1152, 2176

GATHER = ((("y", "z", "x"), 0, 1024), (("z", "x", "y"), 1024, 1024), (("x", "y", "z"), 2048, 1152))
REDUCE = ((("x", "z", "y"), 0, 1280), (("z", "x", "y"), 1280, 1280), (("y", "x", "z"), 2560, 640))

V_IN, V_EXP, V_OUTB, V_SHRB, V_G0, V_G1, V_B0, V_B1, V_ALL = 0, 768, 1792, 2304, 2816, 3328, 3840, 4352, 4864


def where_am_i():
    s = lax.axis_index("section")
    d = lax.axis_index("dp")
    return {"x": d % 4, "z": (d // 4) % 4, "y": (d // 16) * 2 + s}


def chip_id(c):
    return {"section": c["y"] % 2, "dp": (c["y"] // 2) * 16 + c["z"] * 4 + c["x"]}


def moved(c, axis, by):
    return {**c, axis: (c[axis] + by) % 4}


def slots(c, free):
    full = slice(None)
    y = c["y"]
    return ((full, full) if "y" in free else (y % 2, y // 2)) + (
        full if "z" in free else c["z"],
        full if "x" in free else c["x"],
    )


def region(ref, c, free, lo, width):
    return ref.at[slots(c, free) + (slice(None), pl.ds(lo, width))]


def greet(c):
    barrier = pltpu.get_barrier_semaphore()
    for axis in "xyz":
        for by in (1, 2, 3):
            pl.semaphore_signal(barrier, inc=1, device_id=chip_id(moved(c, axis, by)), device_id_type=MESH)
    pl.semaphore_signal(barrier, inc=1, device_id={"tensor": 1 - lax.axis_index("tensor")}, device_id_type=MESH)
    pl.semaphore_wait(barrier, 10)


def push(src, dst, send, recv, target):
    return pltpu.make_async_remote_copy(
        src_ref=src, dst_ref=dst, send_sem=send, recv_sem=recv, device_id=target, device_id_type=MESH
    )


def halves(lo, width):
    first = width // 256 * 128
    return (lo, first), (lo + first, width - first)


class Links:
    def __init__(self, send, recv):
        self.send, self.recv, self.started = send, recv, []

    def go(self, src, dst, at, target):
        copy = push(src, dst, self.send.at[at], self.recv.at[at], chip_id(target))
        copy.start()
        self.started.append(copy)

    def arrived(self, dst, at, source):
        push(dst, dst, self.send.at[at], self.recv.at[at], chip_id(source)).wait_recv()

    def close(self):
        for copy in self.started:
            copy.wait_send()


def gather(held, c, links, meanwhile):
    def spot(p, source, by):
        (_, second, _), lo, width = GATHER[p]
        return region(held, moved(source, second, -by), GATHER[p][0][:1], lo, width)

    def part_of(p, source, by, k):
        (_, second, _), lo, width = GATHER[p]
        return region(held, moved(source, second, -by), GATHER[p][0][:1], *halves(lo, width)[k])

    def send_group(p, at, by):
        for k, way in enumerate((1, 3)):
            to = moved(c, GATHER[p][0][2], way)
            for half in (k, 1 - k):
                src = part_of(p, c, by, half)
                links.go(src, src, (p, 6 + 6 * at + 3 * k + (half != k)), to)

    def forward_group(p, at, by):
        for k, way in enumerate((1, 3)):
            third = GATHER[p][0][2]
            source = moved(c, third, -way)
            src = part_of(p, source, by, k)
            links.arrived(src, (p, 6 + 6 * at + 3 * k), source)
            links.go(src, src, (p, 6 + 6 * at + 3 * k + 2), moved(c, third, way))

    for p, (axes, lo, width) in enumerate(GATHER):
        src = region(held, c, (), lo, width)
        for by in (1, 3, 2):
            links.go(src, src, (p, by - 1), moved(c, axes[0], by))
    meanwhile()
    for p, (axes, lo, width) in enumerate(GATHER):
        for by in (1, 3, 2):
            source = moved(c, axes[0], -by)
            links.arrived(region(held, source, (), lo, width), (p, by - 1), source)
        src = spot(p, c, 0)
        for by in (1, 3, 2):
            links.go(src, src, (p, 2 + by), moved(c, axes[1], by))
    for p in range(3):
        send_group(p, 0, 0)
    order = (0, 1, 3, 2)
    for at in range(1, 4):
        by = order[at]
        for p, (axes, lo, width) in enumerate(GATHER):
            links.arrived(spot(p, c, by), (p, 2 + by), moved(c, axes[1], -by))
            send_group(p, at, by)
        for p in range(3):
            forward_group(p, at - 1, order[at - 1])
    for p in range(3):
        forward_group(p, 3, order[3])
    for at, by in enumerate(order):
        for p, (axes, lo, width) in enumerate(GATHER):
            for k, way in enumerate((1, 3)):
                source, far = moved(c, axes[2], -way), moved(c, axes[2], 2)
                links.arrived(part_of(p, source, by, 1 - k), (p, 6 + 6 * at + 3 * k + 1), source)
                links.arrived(part_of(p, far, by, k), (p, 6 + 6 * at + 3 * k + 2), far)


def add_to(target, terms):
    lead = target.shape[:-2]
    for i in range(int(np.prod(lead))):
        at = tuple(int(k) for k in np.unravel_index(i, lead)) if lead else ()
        value = target[at + (...,)].astype(F32)
        for term in terms:
            value = value + term[at + (...,)].astype(F32)
        target[at + (...,)] = value.astype(BF)


def reduce_shapes():
    shapes = []
    for axes, lo, width in REDUCE:
        groups, last = ((8,), (2,)) if axes[2] == "y" else ((4,), (4,))
        rest = (2, 2) if axes[2] == "y" else (4,)
        shapes += [groups + last + (16, halves(lo, width)[k][1]) for k in range(2)]
        shapes += [groups + last + (16, width)] * 2 + [(3,) + rest + (16, width), (3, 16, width)]
    return shapes


class Reduction:
    order = (2, 1, 3, 0)

    def __init__(self, total, c, bufs, links):
        self.total, self.c, self.bufs, self.links = total, c, bufs, links

    def part(self, p, chip, by, layer, k=None):
        axes, lo, width = REDUCE[p]
        chip = moved(chip, axes[1], by)
        lo, width = (lo, width) if k is None else halves(lo, width)[k]
        if layer is None:
            return region(self.total, chip, axes[2:], lo, width)
        return self.total.at[layer, slice(None), chip["z"], chip["x"], slice(None), pl.ds(lo, width)]

    def at(self, by, layer):
        return self.order.index(by) + 4 * (layer or 0)

    def landing(self, p, by, layer, k, half):
        lo, width = REDUCE[p][1:]
        start, size = halves(lo, width)[half]
        return self.bufs[6 * p + 2 + k].at[self.at(by, layer), :, :, pl.ds(start - lo, size)]

    def open(self, p, layer=None):
        c, axis, links = self.c, REDUCE[p][0][0], self.links
        for by in self.order:
            at = self.at(by, layer)
            for k, way in enumerate((1, 3)):
                to = moved(c, axis, way)
                links.go(self.part(p, moved(c, axis, 2), by, layer, k), self.bufs[6 * p + k].at[at], (p, 6 * at + 3 * k), to)
                links.go(self.part(p, to, by, layer, 1 - k), self.landing(p, by, layer, k, 1 - k), (p, 6 * at + 3 * k + 1), to)

    def middle(self, p, by, layer=None):
        c, axis, links = self.c, REDUCE[p][0][0], self.links
        at = self.at(by, layer)
        for k, way in enumerate((1, 3)):
            to = moved(c, axis, way)
            half = self.bufs[6 * p + k].at[at]
            links.arrived(half, (p, 6 * at + 3 * k), moved(c, axis, -way))
            mine = self.part(p, to, by, layer, k)
            add_to(mine, [half])
            links.go(mine, self.landing(p, by, layer, k, k), (p, 6 * at + 3 * k + 2), to)

    def end(self, p, by, layer=None):
        c, axis, links = self.c, REDUCE[p][0][0], self.links
        at = self.at(by, layer)
        for k, way in enumerate((1, 3)):
            for j, half in ((1, 1 - k), (2, k)):
                links.arrived(self.landing(p, by, layer, k, half), (p, 6 * at + 3 * k + j), moved(c, axis, -way))
        add_to(self.part(p, c, by, layer), [self.bufs[6 * p + 2 + k].at[at] for k in range(2)])

    def second(self, p, by):
        axes, lo, width = REDUCE[p]
        to = moved(self.c, axes[1], by)
        self.links.go(region(self.total, to, axes[2:], lo, width), self.bufs[6 * p + 4].at[by - 1], (p, 47 + by), to)

    def third(self, p):
        axes, lo, width = REDUCE[p]
        terms = [self.bufs[6 * p + 4].at[by - 1] for by in (1, 2, 3)]
        for by in (1, 3, 2):
            self.links.arrived(terms[by - 1], (p, 47 + by), moved(self.c, axes[1], -by))
        add_to(region(self.total, self.c, axes[2:], lo, width), terms)
        for by in (1, 3, 2):
            to = moved(self.c, axes[2], by)
            self.links.go(region(self.total, to, (), lo, width), self.bufs[6 * p + 5].at[by - 1], (p, 50 + by), to)

    def last(self, p):
        axes, lo, width = REDUCE[p]
        terms = [self.bufs[6 * p + 5].at[by - 1] for by in (1, 2, 3)]
        for by in (1, 3, 2):
            self.links.arrived(terms[by - 1], (p, 50 + by), moved(self.c, axes[2], -by))
        add_to(region(self.total, self.c, (), lo, width), terms)


def dot(a, b):
    return jnp.dot(a, b, preferred_element_type=F32)


def dot_nt(a, b):
    return lax.dot_general(a, b, (((1,), (1,)), ((), ())), preferred_element_type=F32)


def weight(held, layer, lo, width):
    return held[layer, :, :, :, :, lo : lo + width].reshape(D, width)


def keep_grad(total, layer, lo, value):
    width = value.shape[-1]
    total[layer, :, :, :, :, lo : lo + width] = value.astype(BF).reshape(2, 4, 4, 16, width)


def vector_maps():
    at = lax.broadcasted_iota(jnp.int32, (1, V_ALL), 1)
    exp_at = at - V_EXP
    wide = at - V_OUTB
    is_in, is_exp = at < V_EXP, at < V_OUTB
    owner = jnp.where(is_in, (at & 63) >> 1, jnp.where(is_exp, (exp_at & 127) >> 2, (wide & 511) >> 4))
    row = jnp.where(is_in, ((at >> 8) << 1) + (at & 1), jnp.where(is_exp, 6 + (exp_at & 3), 10 + (wide >> 9)))
    lane = jnp.where(is_in, (at >> 6) & 3, jnp.where(is_exp, exp_at >> 7, wide & 15))
    return owner, row, lane


ROWS = [(k // 2 * 256, 256) for k in range(6)] + [(V_EXP, 1024)] * 4 + [(V_OUTB + D * k, D) for k in range(6)]


def decode_vectors(held, layer, table):
    owner, row, _ = vector_maps()
    block = held[layer, :, :, :, :, VEC:IN].reshape(32, 16, 128).astype(F32)
    owners = lax.broadcasted_iota(jnp.int32, (32, V_ALL), 0)
    pieces = {}
    for k, (lo, width) in enumerate(ROWS):
        spread = dot(block[:, k, :].astype(BF), table[:, lo : lo + width])
        wanted = jnp.where(row == k, owner, -1)[:, lo : lo + width]
        piece = jnp.sum(jnp.where(owners[:, lo : lo + width] == wanted, spread, 0.0), axis=0, keepdims=True)
        pieces[lo] = piece + pieces[lo] if lo in pieces else piece
    return jnp.concatenate(list(pieces.values()), axis=1)


def encode_vectors(total, layer, me, table, vectors):
    owner, row, lane = vector_maps()
    at = lax.broadcasted_iota(jnp.int32, (1, V_ALL), 1)
    source = jnp.where((at >= V_OUTB) & (at < V_G0), lane >> 3, me)
    owner = jnp.where(source == me, owner, -1)
    owners = lax.broadcasted_iota(jnp.int32, (32, V_ALL), 0)
    rows = []
    for k, (lo, width) in enumerate(ROWS):
        wanted = jnp.where(row == k, owner, -1)[:, lo : lo + width]
        chosen = jnp.where(owners[:, lo : lo + width] == wanted, vectors[:, lo : lo + width], 0.0).astype(BF)
        rows.append(dot_nt(chosen, table[:, lo : lo + width])[:, None, :])
    total[layer, :, :, :, :, VEC:IN] = jnp.concatenate(rows, axis=1).astype(BF).reshape(2, 4, 4, 16, 128)


def rolled(values, by):
    return pltpu.roll(values, by % values.shape[-1], 1)


def turned(values, cosine, sine_front, sine_back):
    return values * cosine + rolled(values, -(ROT // 2)) * sine_front + rolled(values, ROT // 2) * sine_back


def rows_of(i):
    return pl.ds(pl.multiple_of(i * OWN, OWN), OWN)


def project(layer, r, i):
    held, vec = r.held, r.vec
    rows = rows_of(i)
    x = r.x[layer, rows, :].astype(F32)
    middle = jnp.mean(x, axis=-1, keepdims=True)
    center = x - middle
    scale = lax.rsqrt(jnp.mean(center * center, axis=-1, keepdims=True) + EPSILON)
    normal = center * scale
    r.moments[layer, 0, rows, :] = jnp.broadcast_to(middle, (OWN, 128))
    r.moments[layer, 1, rows, :] = jnp.broadcast_to(scale, (OWN, 128))
    first = (normal * vec[layer, :, V_G0:V_G1] + vec[layer, :, V_B0:V_B1]).astype(BF)
    second = (normal * vec[layer, :, V_G1:V_B0] + vec[layer, :, V_B1:V_ALL]).astype(BF)
    r.second[rows, :] = second
    r.first_t[layer, :, rows] = first.T
    r.second_t[layer, :, rows] = second.T
    joint = dot(first, weight(held, layer, IN, 768)) + vec[layer, :, V_IN:V_EXP]
    cosine, front, back = [jnp.concatenate([r.angles[k, rows, :]] * 2, axis=1) for k in range(3)]
    query = turned(joint[:, :256], cosine, front, back).astype(BF) * BF(HD**-0.5)
    key = turned(joint[:, 256:512], cosine, front, back).astype(BF)
    value = joint[:, 512:].astype(BF)
    for k, part in enumerate((query, key, value)):
        part_t = part.T
        for h in range(HEADS):
            r.qkv[layer, k, h, rows, :] = part[:, h * HD : (h + 1) * HD]
            r.qkv_t[layer, k, h, :, rows] = part_t[h * HD : (h + 1) * HD]


def attend(layer, r, h):
    for b in range(2):
        keys = (b + 1) * OWN
        cols = slice(b * OWN, keys)
        scores = dot(r.qkv[layer, 1, h, :keys, :], r.qkv_t[layer, 0, h, :, cols]) + r.mask[:keys, cols]
        powers = jnp.exp(scores - jnp.max(scores, axis=0, keepdims=True))
        shares = (powers * (1.0 / jnp.sum(powers, axis=0, keepdims=True))).astype(BF)
        r.shares[layer, h, :keys, cols] = shares
        r.mixed_t[layer, h, :, cols] = dot(r.qkv_t[layer, 2, h, :, :keys], shares)


def widen(layer, r, i):
    rows = rows_of(i)
    before = dot(r.second[rows, :], weight(r.held, layer, EXP, 1024)) + r.vec[layer, :, V_EXP:V_OUTB]
    chance = 0.5 * (1.0 + lax.erf(before * (0.5**0.5)))
    r.hidden[layer, rows, :] = (before * chance).astype(BF)
    slope = chance + before * jnp.exp(-0.5 * before * before) * ((2.0 * np.pi) ** -0.5)
    r.slope[layer, rows, :] = slope.astype(BF)


def close(layer, r, i):
    rows = rows_of(i)
    branch = dot_nt(r.mixed[layer, rows, :], weight(r.held, layer, OUT, 256))
    branch = branch + dot_nt(r.hidden[layer, rows, :], weight(r.held, layer, SHR, 1024))
    r.away[layer, rows, :] = branch.astype(BF)


def enter(layer, r, i):
    held = r.held
    rows = rows_of(i)
    grad = r.grad[layer, rows, :]
    low = grad.astype(BF)
    r.grad_t[:, rows] = low.T
    mixed_grad = dot(low, weight(held, layer, OUT, 256)).astype(BF)
    mixed_grad_t = mixed_grad.T
    for h in range(HEADS):
        r.mixed_grad[h, rows, :] = mixed_grad[:, h * HD : (h + 1) * HD]
        r.mixed_grad_t[h, :, rows] = mixed_grad_t[h * HD : (h + 1) * HD]
    before = (dot(low, weight(held, layer, SHR, 1024)) * r.slope[layer, rows, :].astype(F32)).astype(BF)
    r.before_grad[rows, :] = before
    r.second_grad[rows, :] = dot_nt(before, weight(held, layer, EXP, 1024))
    return jnp.sum(grad, axis=0, keepdims=True)


def outer_grads(layer, r):
    keep_grad(r.total, layer, OUT, dot(r.grad_t[...], r.mixed[layer]))
    for lo in range(0, 1024, 512):
        keep_grad(r.total, layer, SHR + lo, dot(r.grad_t[...], r.hidden[layer, :, lo : lo + 512]))
        keep_grad(r.total, layer, EXP + lo, dot(r.second_t[layer], r.before_grad[:, lo : lo + 512]))


def attend_back(layer, r, h):
    key_parts, value_parts = [], []
    for b in range(2):
        keys = (b + 1) * OWN
        cols = slice(b * OWN, keys)
        shares = r.shares[layer, h, :keys, cols]
        out_t = r.mixed_grad_t[h, :, cols]
        delta = jnp.sum(out_t.astype(F32) * r.mixed_t[layer, h, :, cols], axis=0, keepdims=True)
        share_grad = dot(r.qkv[layer, 2, h, :keys, :], out_t)
        score_grad = (shares.astype(F32) * (share_grad - delta)).astype(BF)
        r.query_grad_t[h, :, cols] = dot(r.qkv_t[layer, 1, h, :, :keys], score_grad) * (HD**-0.5)
        key_parts.append(dot(score_grad, r.qkv[layer, 0, h, cols, :]))
        value_parts.append(dot(shares, r.mixed_grad[h, cols, :]))
    for k, parts in enumerate((key_parts, value_parts)):
        r.pair_grad[k, h, :OWN, :] = parts[0] + parts[1][:OWN]
        r.pair_grad[k, h, OWN:, :] = parts[1][OWN:]


def join(layer, r, i):
    vec = r.vec
    rows = rows_of(i)
    cosine, front, back = [jnp.concatenate([r.angles[k, rows, :]] * 2, axis=1) for k in range(3)]
    query = r.query_grad_t[:, :, rows].reshape(HEADS * HD, OWN).T
    key = jnp.concatenate([r.pair_grad[0, h, rows, :] for h in range(HEADS)], axis=1)
    value = jnp.concatenate([r.pair_grad[1, h, rows, :] for h in range(HEADS)], axis=1)
    query = turned(query, cosine, -front, -back)
    key = turned(key, cosine, -front, -back)
    joint = jnp.concatenate([query, key, value], axis=1).astype(BF)
    r.joint_grad[rows, :] = joint
    first_grad = dot_nt(joint, weight(r.held, layer, IN, 768))
    second_grad = r.second_grad[rows, :]
    middle, scale = [jnp.concatenate([r.moments[layer, k, rows, :]] * 4, axis=1) for k in range(2)]
    normal = (r.x[layer, rows, :].astype(F32) - middle) * scale
    scaled = first_grad * vec[layer, :, V_G0:V_G1] + second_grad * vec[layer, :, V_G1:V_B0]
    passed = scaled - jnp.mean(scaled, axis=-1, keepdims=True)
    passed = passed - normal * jnp.mean(scaled * normal, axis=-1, keepdims=True)
    r.away[3 - layer, rows, :] = (passed * scale).astype(BF)
    terms = [joint.astype(F32), r.before_grad[rows, :].astype(F32)]
    terms += [first_grad * normal, second_grad * normal, first_grad, second_grad]
    return [jnp.sum(term, axis=0, keepdims=True) for term in terms]


def inner_grads(layer, r, out_sum, sums):
    keep_grad(r.total, layer, IN, dot(r.first_t[layer], r.joint_grad[...]))
    vectors = jnp.concatenate([sums[0], sums[1], out_sum, out_sum, *sums[2:]], axis=1)
    encode_vectors(r.total, layer, r.me, r.table, vectors)


class Refs:
    pass


SCRATCH = dict(
    held=((2, 2, 4, 4, 16, COLS), BF),
    total=((2, 2, 4, 4, 16, COLS), BF),
    vec=((2, 1, V_ALL), F32),
    table=((128, V_ALL), BF),
    x=((2, LEN, D), BF),
    cot=((LEN, D), BF),
    grad=((2, LEN, D), F32),
    moments=((2, 2, LEN, 128), F32),
    first_t=((2, D, LEN), BF),
    second_t=((2, D, LEN), BF),
    qkv=((2, 3, HEADS, LEN, HD), BF),
    qkv_t=((2, 3, HEADS, HD, LEN), BF),
    shares=((2, HEADS, LEN, LEN), BF),
    mixed_t=((2, HEADS, HD, LEN), F32),
    mixed=((2, LEN, HEADS * HD), BF),
    hidden=((2, LEN, 1024), BF),
    slope=((2, LEN, 1024), BF),
    mask=((LEN, LEN), F32),
    angles=((3, LEN, 128), F32),
    away=((4, LEN, D), BF),
    come=((4, LEN, D), BF),
    second=((LEN, D), BF),
    grad_t=((D, LEN), BF),
    mixed_grad=((HEADS, LEN, HD), BF),
    mixed_grad_t=((HEADS, HD, LEN), BF),
    before_grad=((LEN, 1024), BF),
    second_grad=((LEN, D), F32),
    query_grad_t=((HEADS, HD, LEN), F32),
    pair_grad=((2, HEADS, LEN, HD), F32),
    joint_grad=((LEN, 768), BF),
    states=((2, OWN, D), BF),
    grads=((2, OWN, D), F32),
    grads_low=((2, OWN, D), BF),
    states_in=((OWN, D), BF),
    grads_in=((OWN, D), BF),
    small=((16, 128), F32),
    small_in=((16, 128), F32),
    small_out=((16, 128), F32),
    small_back=((16, 128), F32),
)


def rotary_tables(angles, r):
    lane = lax.broadcasted_iota(jnp.int32, (1, 128), 1) & (HD - 1)
    rates = jnp.zeros((1, 128), F32)
    for j in range(ROT // 2):
        rates = jnp.where((lane < ROT) & ((lane & 7) == j), 10000.0 ** (-2.0 * j / ROT), rates)
    angles = angles * rates
    sine = jnp.sin(angles)
    r.angles[0] = jnp.cos(angles)
    r.angles[1] = jnp.where(lane < ROT // 2, -sine, 0.0)
    r.angles[2] = jnp.where((lane >= ROT // 2) & (lane < ROT), sine, 0.0)


def kernel(inward, inward_b, outward, outward_b, expand, expand_b, shrink, shrink_b, gains, shifts, *rest):
    x_in, cot_in, labels, places, states_out, grads_out, weights_out, vectors_out, *scratch = rest
    r = Refs()
    names = list(SCRATCH)
    for name, ref in zip(names, scratch):
        setattr(r, name, ref)
    gather_send, gather_recv, reduce_send, reduce_recv, near_send, near_recv, own_sem = scratch[len(names) : len(names) + 7]
    bufs = scratch[len(names) + 7 :]
    c = where_am_i()
    section = lax.axis_index("section")
    me = r.me = lax.axis_index("tensor")
    other = {"tensor": 1 - me}
    mine, theirs = rows_of(me), rows_of(1 - me)

    def near(k, src, dst):
        return push(src, dst, near_send.at[k], near_recv.at[k], other)

    def side(k, src, dst):
        return push(src, dst, near_send.at[k], near_recv.at[k], {"section": 1 - section})

    greet(c)
    held = r.held
    own_slot = slots(c, ())
    small = r.small
    small[...] = jnp.zeros((16, 128), F32)
    for j in range(3):
        small[2 * j : 2 * j + 2, :HEADS] = inward_b[0, j].astype(F32)
    small[6:10, :8] = expand_b[0].astype(F32)
    for t in range(2):
        for at, part in ((10, outward_b[...]), (11, shrink_b[...]), (12, gains[0]), (14, shifts[0])):
            small[at : at + part.shape[0], 8 * t : 8 * t + 8] = jnp.where(me == t, part.astype(F32), 0.0)
    first = near(0, small, r.small_in)
    first.start()

    def pack(lo, value):
        held[own_slot + (slice(None), slice(lo, lo + value.shape[-1]))] = value

    for j in range(3):
        pack(IN + 256 * j, inward[0, j])
    pack(OUT, outward[0])
    pack(EXP, expand[0])
    pack(SHR, shrink[0])
    first.wait()
    row_at = lax.broadcasted_iota(jnp.int32, (16, 128), 0)
    pack(VEC, (small[...] + jnp.where(row_at >= 10, r.small_in[...], 0.0)).astype(BF))
    pairs = [near(1, x_in.at[section], r.x.at[0, mine]), near(2, cot_in.at[section], r.cot.at[mine])]
    owns = [
        pltpu.make_async_copy(x_in.at[section], r.x.at[0, mine], own_sem.at[0]),
        pltpu.make_async_copy(cot_in.at[section], r.cot.at[mine], own_sem.at[1]),
    ]

    def meanwhile():
        for copy in pairs + owns:
            copy.start()
        _, _, lane = vector_maps()
        r.table[...] = (lax.broadcasted_iota(jnp.int32, (128, V_ALL), 0) == lane).astype(F32).astype(BF)

    links = Links(gather_send, gather_recv)
    gather(held, c, links, meanwhile)
    label = labels[pl.ds(section, 1), :].astype(F32)
    place = places[pl.ds(section, 1), :].astype(F32)
    rotary_tables(jnp.broadcast_to(place, (128, LEN)).T, r)
    label_t = jnp.concatenate([jnp.broadcast_to(label, (128, LEN)).T] * 4, axis=1)
    key_at = lax.broadcasted_iota(jnp.int32, (LEN, LEN), 0)
    query_at = lax.broadcasted_iota(jnp.int32, (LEN, LEN), 1)
    r.mask[...] = jnp.where((key_at <= query_at) & (label_t == label), 0.0, MASKED)
    for layer in range(2):
        r.vec[layer] = decode_vectors(held, layer, r.table)
    for copy in pairs + owns:
        copy.wait()
    links.close()

    def swap(k, rows, sem):
        copy = near(sem, r.away.at[k, rows], r.come.at[k, rows])
        copy.start()
        return copy

    def finish(layer, rows):
        bias = r.vec[layer, :, V_OUTB:V_SHRB] + r.vec[layer, :, V_SHRB:V_G0]
        both = r.away[layer, rows, :].astype(F32) + r.come[layer, rows, :].astype(F32)
        return (r.x[layer, rows, :].astype(F32) + both + bias).astype(BF)

    halves_of = [slice(0, OWN), slice(OWN, LEN)]
    swaps = []
    for layer in range(2):
        for i in range(2):
            if layer == 1:
                swaps[i].wait()
                r.x[1, halves_of[i], :] = finish(0, halves_of[i])
            project(layer, r, i)
        for h in range(HEADS):
            attend(layer, r, h)
        r.mixed[layer] = r.mixed_t[layer].reshape(HEADS * HD, LEN).T.astype(BF)
        for i in range(2):
            widen(layer, r, i)
            close(layer, r, i)
            if layer == 0:
                swaps.append(swap(0, halves_of[i], 3 + i))
    r.states[0] = finish(0, mine)
    state_swap = swap(1, theirs, 5)

    links = Links(reduce_send, reduce_recv)
    sums_of = Reduction(r.total, c, bufs, links)
    sides = []
    r.grad[1] = r.cot[...].astype(F32)
    for layer in (1, 0):
        out_sum = jnp.zeros((1, D), F32)
        for i in range(2):
            if layer == 0:
                swaps[i].wait()
                rows = halves_of[i]
                both = r.away[2, rows, :].astype(F32) + r.come[2, rows, :].astype(F32)
                r.grad[0, rows, :] = (r.grad[1, rows, :] + both).astype(BF).astype(F32)
            out_sum = out_sum + enter(layer, r, i)
        if layer == 1:
            state_swap.wait()
            r.states[1] = finish(1, mine)
        else:
            both = r.away[2, mine, :].astype(F32) + r.come[2, mine, :].astype(F32)
            r.grads[1] = r.grad[1, mine, :] + both
        outer_grads(layer, r)
        if layer == 0:
            for by in sums_of.order:
                for p in range(2):
                    sums_of.middle(p, by, 1)
        for h in range(HEADS):
            attend_back(layer, r, h)
        sums = None
        swaps = []
        for i in range(2):
            more = join(layer, r, i)
            sums = more if sums is None else [a + b for a, b in zip(sums, more)]
            if layer == 1:
                swaps.append(swap(2, halves_of[i], 6 + i))
        if layer == 0:
            swaps.append(swap(3, theirs, 8))
        inner_grads(layer, r, out_sum, sums)
        if layer == 1:
            for p in range(2):
                sums_of.open(p, 1)
            sides.append(side(9, r.states.at[1 - section], r.states_in))
            sides[0].start()
    sums_of.open(2)
    for p in range(2):
        sums_of.open(p, 0)
    for by in sums_of.order:
        for p in range(2):
            sums_of.end(p, by, 1)
    swaps[0].wait()
    both = r.away[3, mine, :].astype(F32) + r.come[3, mine, :].astype(F32)
    r.grads[0] = r.grad[0, mine, :] + both
    r.grads_low[...] = r.grads[...].astype(BF)
    for by in sums_of.order:
        sums_of.middle(2, by)
        for p in range(2):
            sums_of.middle(p, by, 0)
    states_out[section] = r.states[section]
    grads_out[section] = r.grads[section]
    for by in sums_of.order:
        for p in range(3):
            sums_of.end(p, by, 0 if p < 2 else None)
            if by:
                sums_of.second(p, by)
    sides.append(side(10, r.grads_low.at[1 - section], r.grads_in))
    sides[1].start()
    for p in range(3):
        sums_of.third(p)
    for p in range(3):
        sums_of.last(p)
    own = r.total[own_slot].astype(F32)
    weights_out[...] = own[:, IN:]
    r.small_out[...] = own[:, VEC:IN]
    last = near(11, r.small_out, r.small_back)
    last.start()
    for copy in sides:
        copy.wait()
    states_out[1 - section] = r.states_in[...]
    grads_out[1 - section] = r.grads_in[...].astype(F32)
    links.close()
    last.wait()
    value = r.small_out[...] + jnp.where(row_at >= 12, r.small_back[...], 0.0)
    vectors_out[...] = jnp.where((row_at >= 10) & (me == 0), pltpu.roll(value, 8, 1), value)


def unpack(states, grads, weights, vectors, *rest):
    states_out, grads_out, gains, shifts, inward, inward_b, outward, outward_b, expand, expand_b, shrink, shrink_b = rest
    states_out[0] = states[...]
    grads_out[0] = grads[...]
    for j in range(3):
        inward[0, j] = weights[:, 256 * j : 256 * (j + 1)]
    outward[0] = weights[:, OUT - IN : EXP - IN]
    expand[0] = weights[:, EXP - IN : SHR - IN]
    shrink[0] = weights[:, SHR - IN :]
    for j in range(3):
        inward_b[0, j] = vectors[2 * j : 2 * j + 2, :HEADS]
    expand_b[0] = vectors[6:10, :8]
    outward_b[...] = vectors[10:11, 8:16]
    shrink_b[...] = vectors[11:12, 8:16]
    gains[0] = vectors[12:14, 8:16]
    shifts[0] = vectors[14:16, 8:16]


def local(
    block_input,
    out_cotangent,
    segments,
    positions,
    norm_gains,
    norm_shifts,
    inward_weight,
    inward_bias,
    outward_weight,
    outward_bias,
    expand_weight,
    expand_bias,
    shrink_weight,
    shrink_bias,
):
    swapped = lambda array: jnp.swapaxes(array, -1, -2)
    vmem = pl.BlockSpec(memory_space=pltpu.VMEM)
    anywhere = pl.BlockSpec(memory_space=pl.ANY)
    dma = pltpu.SemaphoreType.DMA
    results = pl.pallas_call(
        kernel,
        out_shape=(
            jax.ShapeDtypeStruct((2, OWN, D), BF),
            jax.ShapeDtypeStruct((2, OWN, D), F32),
            jax.ShapeDtypeStruct((16, COLS - IN), F32),
            jax.ShapeDtypeStruct((16, 128), F32),
        ),
        in_specs=[vmem] * 10 + [anywhere] * 2 + [vmem] * 2,
        out_specs=(vmem,) * 4,
        scratch_shapes=[pltpu.VMEM(shape, kind) for shape, kind in SCRATCH.values()]
        + [dma((3, 30)), dma((3, 30)), dma((3, 54)), dma((3, 54)), dma((12,)), dma((12,)), dma((2,))]
        + [pltpu.VMEM(shape, BF) for shape in reduce_shapes()],
        compiler_params=pltpu.CompilerParams(collective_id=0, has_side_effects=True, vmem_limit_bytes=62 << 20),
    )(
        jnp.swapaxes(inward_weight, 1, 2),
        swapped(inward_bias),
        swapped(outward_weight),
        outward_bias,
        expand_weight,
        swapped(expand_bias),
        swapped(shrink_weight),
        shrink_bias,
        norm_gains,
        norm_shifts,
        block_input,
        out_cotangent,
        segments,
        positions,
    )
    out_shapes = [(1, 2, OWN, D), (1, 2, OWN, D), (1, 2, 8), (1, 2, 8), (1, 3, 16, 256), (1, 3, 2, 4)]
    out_shapes += [(1, 16, 256), (1, 8), (1, 16, 1024), (1, 4, 8), (1, 16, 1024), (1, 8)]
    outs = pl.pallas_call(
        unpack,
        out_shape=tuple(jax.ShapeDtypeStruct(shape, BF if k == 0 else F32) for k, shape in enumerate(out_shapes)),
        in_specs=[vmem] * 4,
        out_specs=(vmem,) * 12,
    )(*results)
    states, grads, gains, shifts, inward, inward_b, outward, outward_b, expand, expand_b, shrink, shrink_b = outs
    inward = jnp.swapaxes(inward, 1, 2)
    outward, shrink, inward_b, expand_b = [swapped(array) for array in (outward, shrink, inward_b, expand_b)]
    return (states, grads, gains, shifts, inward, inward_b, outward, outward_b, expand, expand_b, shrink, shrink_b)


def solution(mesh):
    return jax.shard_map(
        local,
        mesh=mesh,
        in_specs=(
            P(None, ("dp", "tensor"), None),
            P(None, ("dp", "tensor"), None),
            P(None, "dp"),
            P(None, "dp"),
            P("section", None, ("dp", "tensor")),
            P("section", None, ("dp", "tensor")),
            P("section", "dp", None, "tensor"),
            P("section", None, "tensor", "dp"),
            P("section", "tensor", "dp"),
            P("section", ("dp", "tensor")),
            P("section", "dp", "tensor"),
            P("section", "tensor", "dp"),
            P("section", "tensor", "dp"),
            P("section", ("dp", "tensor")),
        ),
        out_specs=(
            P("section", None, ("dp", "tensor"), None),
            P("section", None, ("dp", "tensor"), None),
            P("section", None, ("dp", "tensor")),
            P("section", None, ("dp", "tensor")),
            P("section", "dp", None, "tensor"),
            P("section", None, "tensor", "dp"),
            P("section", "tensor", "dp"),
            P("section", ("dp", "tensor")),
            P("section", "dp", "tensor"),
            P("section", "tensor", "dp"),
            P("section", "tensor", "dp"),
            P("section", ("dp", "tensor")),
        ),
        check_vma=False,
    )
```

time: 161 us -> 115 us (0.71)
  Pallas kernels: 140 us -> 114 us
  local copies, waits for them, and re-layouts: 17.6 us -> 0 us
  other arithmetic: 2.03 us -> 0 us
    pallas_call x1, Pallas kernels: 140 us -> 112 us  [local(): pl.pallas_call(kernel, out_shape=(jax.ShapeDtypeStruct((2, OWN, D), BF),...]
    unnamed x49 -> x0, local copies, waits for them, and re-layouts: 7.68 us -> none
    slice x5 -> x0, local copies, waits for them, and re-layouts: 4.24 us -> none  [the longest x1 1.27 us: local(): vec[64:72].reshape(1, 8)]
    broadcast_in_dim x3 -> x0, local copies, waits for them, and re-layouts: 3.71 us -> none  [the longest x1 1.53 us: local(): weights[:, SHR:VEC].T[None]]
    pallas_call x0 -> x1, Pallas kernels: none -> 2.7 us  [local(): pl.pallas_call(unpack, out_shape=tuple((jax.ShapeDtypeStruct(shape, BF if...]
    reshape x9 -> x0, local copies, waits for them, and re-layouts: 1.82 us -> none  [the longest x1 0.64 us: local(): vec[88:104].reshape(1, 2, 8)]
where the time goes in v2:
time: 115 us
  Pallas kernels  114 us (99%)
    pallas_call x1, Pallas kernels, local(): pl.pallas_call(kernel, out_shape=(jax.ShapeDtypeStruct((2, OWN, D), BF),...  112 us
    pallas_call x1, Pallas kernels, local(): pl.pallas_call(unpack, out_shape=tuple((jax.ShapeDtypeStruct(shape, BF if...  2.7 us

profile of v2, /device:TPU:1, one launch (start us, length us, event | category | flops | bytes accessed | tf_op | source)
XLA Modules:
  0.0 115.1 jit_solution(6339030472648807405)
XLA Ops:
  0.6 111.6 %shard_map.229 = (bf16[2,256,512]{2,1,0:T(8,128)(2,1)}, f32[2,256,512]{2,1,0:T(8,128)}, f32[16,3072]{1,0:T(8,128)}, f32[16,128]{1,0:T(8,128)}) custom-call(bf16[1,3,16,256]{3,2,1,0:T(8,128)(2,1)} %bitcast.11, bf16[1,3,2,4]{3,2,1,0:T(2,128)(2,1)} %bitcast.13, bf16[1,16,256]{2,1,0:T(8,128)(2,1)} %bitcast.12, bf16[1,8]{1,0:T(2,128)(2,1)} %outward_b.1, ...), custom_call_target="tpu_custom_call" | custom-call | tf_op jit(solution)/shard_map/pallas_call | solution.py:720
  112.2 2.7 %shard_map.230 = (bf16[1,2,256,512]{3,2,1,0:T(8,128)(2,1)}, f32[1,2,256,512]{3,2,1,0:T(8,128)}, f32[1,2,8]{2,1,0:T(2,128)}, f32[1,2,8]{2,1,0:T(2,128)}, f32[1,3,...) custom-call(bf16[2,256,512]{2,1,0:T(8,128)(2,1)} %get-tuple-element., ...), custom_call_target="tpu_custom_call" | custom-call | tf_op jit(solution)/shard_map/pallas_call | solution.py:752

commit v3 on v2

--- a/solution.py
+++ b/solution.py
@@ -22,7 +22,12 @@
 VEC, IN, OUT, EXP, SHR = 0, 128, 896, 1152, 2176
 
 GATHER = ((("y", "z", "x"), 0, 1024), (("z", "x", "y"), 1024, 1024), (("x", "y", "z"), 2048, 1152))
-REDUCE = ((("x", "z", "y"), 0, 1280), (("z", "x", "y"), 1280, 1280), (("y", "x", "z"), 2560, 640))
+REDUCE = (
+    (("x", "z", "y"), 1024, 1408),
+    (("z", "x", "y"), 0, 1024),
+    (("y", "x", "z"), 2432, 384),
+    (("y", "z", "x"), 2816, 384),
+)
 
 V_IN, V_EXP, V_OUTB, V_SHRB, V_G0, V_G1, V_B0, V_B1, V_ALL = 0, 768, 1792, 2304, 2816, 3328, 3840, 4352, 4864
 
@@ -91,7 +96,7 @@
             copy.wait_send()
 
 
-def gather(held, c, links, meanwhile):
+def gather(held, c, links, pack_vectors, meanwhile):
     def spot(p, source, by):
         (_, second, _), lo, width = GATHER[p]
         return region(held, moved(source, second, -by), GATHER[p][0][:1], lo, width)
@@ -115,7 +120,9 @@
             links.arrived(src, (p, 6 + 6 * at + 3 * k), source)
             links.go(src, src, (p, 6 + 6 * at + 3 * k + 2), moved(c, third, way))
 
-    for p, (axes, lo, width) in enumerate(GATHER):
+    for p, (axes, lo, width) in reversed(list(enumerate(GATHER))):
+        if p == 0:
+            pack_vectors()
         src = region(held, c, (), lo, width)
         for by in (1, 3, 2):
             links.go(src, src, (p, by - 1), moved(c, axes[0], by))
@@ -537,9 +544,11 @@
     pack(OUT, outward[0])
     pack(EXP, expand[0])
     pack(SHR, shrink[0])
-    first.wait()
     row_at = lax.broadcasted_iota(jnp.int32, (16, 128), 0)
-    pack(VEC, (small[...] + jnp.where(row_at >= 10, r.small_in[...], 0.0)).astype(BF))
+
+    def pack_vectors():
+        first.wait()
+        pack(VEC, (small[...] + jnp.where(row_at >= 10, r.small_in[...], 0.0)).astype(BF))
     pairs = [near(1, x_in.at[section], r.x.at[0, mine]), near(2, cot_in.at[section], r.cot.at[mine])]
     owns = [
         pltpu.make_async_copy(x_in.at[section], r.x.at[0, mine], own_sem.at[0]),
@@ -552,15 +561,16 @@
         _, _, lane = vector_maps()
         r.table[...] = (lax.broadcasted_iota(jnp.int32, (128, V_ALL), 0) == lane).astype(F32).astype(BF)
 
+        label = labels[pl.ds(section, 1), :].astype(F32)
+        place = places[pl.ds(section, 1), :].astype(F32)
+        rotary_tables(jnp.broadcast_to(place, (128, LEN)).T, r)
+        label_t = jnp.concatenate([jnp.broadcast_to(label, (128, LEN)).T] * 4, axis=1)
+        key_at = lax.broadcasted_iota(jnp.int32, (LEN, LEN), 0)
+        query_at = lax.broadcasted_iota(jnp.int32, (LEN, LEN), 1)
+        r.mask[...] = jnp.where((key_at <= query_at) & (label_t == label), 0.0, MASKED)
+
     links = Links(gather_send, gather_recv)
-    gather(held, c, links, meanwhile)
-    label = labels[pl.ds(section, 1), :].astype(F32)
-    place = places[pl.ds(section, 1), :].astype(F32)
-    rotary_tables(jnp.broadcast_to(place, (128, LEN)).T, r)
-    label_t = jnp.concatenate([jnp.broadcast_to(label, (128, LEN)).T] * 4, axis=1)
-    key_at = lax.broadcasted_iota(jnp.int32, (LEN, LEN), 0)
-    query_at = lax.broadcasted_iota(jnp.int32, (LEN, LEN), 1)
-    r.mask[...] = jnp.where((key_at <= query_at) & (label_t == label), 0.0, MASKED)
+    gather(held, c, links, pack_vectors, meanwhile)
     for layer in range(2):
         r.vec[layer] = decode_vectors(held, layer, r.table)
     for copy in pairs + owns:
@@ -612,14 +622,18 @@
         if layer == 1:
             state_swap.wait()
             r.states[1] = finish(1, mine)
+            sides.append(side(9, r.states.at[1 - section], r.states_in))
+            sides[0].start()
         else:
             both = r.away[2, mine, :].astype(F32) + r.come[2, mine, :].astype(F32)
             r.grads[1] = r.grad[1, mine, :] + both
         outer_grads(layer, r)
         if layer == 0:
             for by in sums_of.order:
-                for p in range(2):
-                    sums_of.middle(p, by, 1)
+                sums_of.middle(0, by, 1)
+            sums_of.open(2)
+            sums_of.open(3)
+        sums_of.open(0, layer)
         for h in range(HEADS):
             attend_back(layer, r, h)
         sums = None
@@ -632,37 +646,40 @@
         if layer == 0:
             swaps.append(swap(3, theirs, 8))
         inner_grads(layer, r, out_sum, sums)
-        if layer == 1:
-            for p in range(2):
-                sums_of.open(p, 1)
-            sides.append(side(9, r.states.at[1 - section], r.states_in))
-            sides[0].start()
-    sums_of.open(2)
-    for p in range(2):
-        sums_of.open(p, 0)
+        sums_of.open(1, layer)
     for by in sums_of.order:
-        for p in range(2):
-            sums_of.end(p, by, 1)
+        sums_of.middle(1, by, 1)
+    for by in sums_of.order:
+        sums_of.middle(2, by)
+        sums_of.middle(3, by)
+        sums_of.middle(0, by, 0)
     swaps[0].wait()
     both = r.away[3, mine, :].astype(F32) + r.come[3, mine, :].astype(F32)
     r.grads[0] = r.grad[0, mine, :] + both
     r.grads_low[...] = r.grads[...].astype(BF)
     for by in sums_of.order:
-        sums_of.middle(2, by)
-        for p in range(2):
-            sums_of.middle(p, by, 0)
+        sums_of.end(0, by, 1)
+    for by in sums_of.order:
+        sums_of.middle(1, by, 0)
     states_out[section] = r.states[section]
     grads_out[section] = r.grads[section]
     for by in sums_of.order:
-        for p in range(3):
-            sums_of.end(p, by, 0 if p < 2 else None)
-            if by:
+        sums_of.end(2, by)
+        sums_of.end(3, by)
+        sums_of.end(0, by, 0)
+        if by:
+            for p in (2, 3, 0):
                 sums_of.second(p, by)
+    for by in sums_of.order:
+        sums_of.end(1, by, 1)
+        sums_of.end(1, by, 0)
+        if by:
+            sums_of.second(1, by)
     sides.append(side(10, r.grads_low.at[1 - section], r.grads_in))
     sides[1].start()
-    for p in range(3):
+    for p in (2, 3, 0, 1):
         sums_of.third(p)
-    for p in range(3):
+    for p in (2, 3, 0, 1):
         sums_of.last(p)
     own = r.total[own_slot].astype(F32)
     weights_out[...] = own[:, IN:]
@@ -728,7 +745,7 @@
         in_specs=[vmem] * 10 + [anywhere] * 2 + [vmem] * 2,
         out_specs=(vmem,) * 4,
         scratch_shapes=[pltpu.VMEM(shape, kind) for shape, kind in SCRATCH.values()]
-        + [dma((3, 30)), dma((3, 30)), dma((3, 54)), dma((3, 54)), dma((12,)), dma((12,)), dma((2,))]
+        + [dma((3, 30)), dma((3, 30)), dma((4, 54)), dma((4, 54)), dma((12,)), dma((12,)), dma((2,))]
         + [pltpu.VMEM(shape, BF) for shape in reduce_shapes()],
         compiler_params=pltpu.CompilerParams(collective_id=0, has_side_effects=True, vmem_limit_bytes=62 << 20),
     )(

time: 115 us -> 112 us (0.974)
  Pallas kernels: 114 us -> 111 us
    pallas_call x1, Pallas kernels: 112 us -> 109 us  [local(): pl.pallas_call(kernel, out_shape=(jax.ShapeDtypeStruct((2, OWN, D), BF),...]
where the time goes in v3:
time: 112 us
  Pallas kernels  111 us (99%)
    pallas_call x1, Pallas kernels, local(): pl.pallas_call(kernel, out_shape=(jax.ShapeDtypeStruct((2, OWN, D), BF),...  109 us
    pallas_call x1, Pallas kernels, local(): pl.pallas_call(unpack, out_shape=tuple((jax.ShapeDtypeStruct(shape, BF if...  2.7 us

profile of v3, /device:TPU:1, one launch (start us, length us, event | category | flops | bytes accessed | tf_op | source)
XLA Modules:
  0.0 112.2 jit_solution(6403545004541066745)
XLA Ops:
  0.6 108.7 %shard_map.229 = (bf16[2,256,512]{2,1,0:T(8,128)(2,1)}, f32[2,256,512]{2,1,0:T(8,128)}, f32[16,3072]{1,0:T(8,128)}, f32[16,128]{1,0:T(8,128)}) custom-call(bf16[1,3,16,256]{3,2,1,0:T(8,128)(2,1)} %bitcast.11, bf16[1,3,2,4]{3,2,1,0:T(2,128)(2,1)} %bitcast.13, bf16[1,16,256]{2,1,0:T(8,128)(2,1)} %bitcast.12, bf16[1,8]{1,0:T(2,128)(2,1)} %outward_b.1, ...), custom_call_target="tpu_custom_call" | custom-call | tf_op jit(solution)/shard_map/pallas_call | solution.py:737
  109.4 2.7 %shard_map.230 = (bf16[1,2,256,512]{3,2,1,0:T(8,128)(2,1)}, f32[1,2,256,512]{3,2,1,0:T(8,128)}, f32[1,2,8]{2,1,0:T(2,128)}, f32[1,2,8]{2,1,0:T(2,128)}, f32[1,3,...) custom-call(bf16[2,256,512]{2,1,0:T(8,128)(2,1)} %get-tuple-element., ...), custom_call_target="tpu_custom_call" | custom-call | tf_op jit(solution)/shard_map/pallas_call | solution.py:769
